TPU v7x, 512 devices: a whole 4x8x8 slice. The times are simulated.
512 devices in a mesh: field: 2 (over core), group: 8 (over y), row: 32 (over z, x).
Axes of the slice: x: 4, y: 8, z: 8, core: 2. Of those that a mesh axis runs over, the one named last changes fastest.
Arguments:
- anomalies: bfloat16 [2, 262144, 512], P('field', ('group', 'row')), may hold values from -6 to 6
- valid_rows: int32 [2, 256], P('field', ('group', 'row')), may hold values from 512 to 1024
- start_basis: float32 [512, 64], replicated, may hold values from -6 to 6
Outputs:
- patterns: float32 [2, 262144, 64], P('field', ('group', 'row'))
- strengths: float32 [64], replicated
Inputs may be any that keep to these rules, and one draw needn't show every extreme that they name: `valid_rows`: the number of ocean points at the head of each shard; the rest of the shard is land and holds values that must be ignored.
All inputs are finite; a program needn't handle non-finite values.
Results may differ from a plain program's by a relative error of at most 0.0003.
Values sent between devices are 32-bit elements; how exact they have to be, the bound alone decides.
A program may use at most 64 MiB of HBM per device.

v0:
```python
import jax
import jax.numpy as jnp
from jax import lax
from jax.sharding import Mesh
from jax.sharding import PartitionSpec as P

GROUP_ROW = ("group", "row_0", "row_1")


HIGH = lax.Precision.HIGHEST


def cut_along(value, dim, devices):
    before, after = (value.shape[:dim], value.shape[dim + 1 :])
    return jnp.moveaxis(value.reshape(*before, devices, -1, *after), dim, 0)


def sent_and_summed(value, axis, dim):
    devices = lax.axis_size(axis)
    pieces = lax.all_to_all(cut_along(value, dim, devices), axis, 0, 0, tiled=True)
    return jnp.sum(pieces, axis=0)


def summed_rows(value, axes, dim):
    far, near = axes
    own = sent_and_summed(cut_along(value, dim, lax.axis_size(far)), near, dim + 1)
    return jnp.sum(lax.all_to_all(own, far, 0, 0, tiled=True), axis=0)


def padded_to(lines, devices):
    spare = -lines.shape[0] % devices
    if not spare:
        return lines
    return jnp.concatenate([lines, jnp.zeros((spare, *lines.shape[1:]), lines.dtype)])


def copy_for_each(value, axis):
    copies = jnp.broadcast_to(value, (lax.axis_size(axis), *value.shape))
    return lax.all_to_all(copies, axis, split_axis=0, concat_axis=0, tiled=True)


def joined_along(pieces, dim):
    pieces = jnp.moveaxis(pieces, 0, dim)
    shape = pieces.shape
    return pieces.reshape(*shape[:dim], shape[dim] * shape[dim + 1], *shape[dim + 2 :])


def gathered_by_axis(value, axes, dim):
    far, near = axes
    leading = copy_for_each(value, far)
    pieces = jnp.swapaxes(copy_for_each(leading, near), 0, 1)
    return joined_along(pieces.reshape(-1, *value.shape), dim)


def total_of(value, axes):
    own = summed_rows(padded_to(value, lax.axis_size(axes[0]) * lax.axis_size(axes[1])), axes, 0)
    whole = gathered_by_axis(own, axes, 0)
    return whole[: len(value)].reshape(value.shape)


def packed_total(arrays, axis):
    vector, at, finished = (jnp.concatenate([a.reshape(-1) for a in arrays]), 0, [])
    total = total_of(vector, axis)
    for a in arrays:
        finished.append(total[at : at + a.size].reshape(a.shape))
        at += a.size
    return tuple(finished)


def from_partner(value, axis, apart):
    return lax.ppermute(value, axis, [(i, i ^ 1 << apart) for i in range(lax.axis_size(axis))])


def orthonormal(block):
    product = jnp.dot(block.T, block, precision=HIGH, preferred_element_type=jnp.float32)
    lower = jnp.linalg.cholesky(product)
    return lax.linalg.triangular_solve(lower, block, left_side=False, lower=True, transpose_a=True)


def per_device(anomalies, valid_rows, start_basis):
    values = anomalies[0]
    rows_here = values.shape[0]
    ocean = valid_rows[0, 0]
    place = lax.broadcasted_iota(jnp.int32, (rows_here, 1), 0)
    masked = jnp.where(place < ocean, values, jnp.zeros_like(values))
    gram = lax.dot_general(
        masked, masked, (((0,), (0,)), ((), ())), preferred_element_type=jnp.float32
    )
    count = ocean.astype(jnp.float32)
    gram, count = packed_total((gram, count), (("group", "row_0"), "row_1"))
    lower = jnp.linalg.cholesky(gram / count)
    factor = lower.T
    which = lax.axis_index("field")
    other = from_partner(factor, "field", 0)
    first = jnp.where(which == 0, factor, other)
    second = jnp.where(which == 0, other, factor)
    coupling = jnp.dot(first, second.T, precision=HIGH, preferred_element_type=jnp.float32)
    right = start_basis
    left = orthonormal(jnp.dot(coupling, right, precision=HIGH, preferred_element_type=jnp.float32))
    right = orthonormal(
        jnp.dot(coupling.T, left, precision=HIGH, preferred_element_type=jnp.float32)
    )
    image = jnp.dot(coupling, right, precision=HIGH, preferred_element_type=jnp.float32)
    strengths = jnp.sum(left * image, axis=0)
    chosen = jnp.where(which == 0, left, right)
    solved = lax.linalg.triangular_solve(
        lower, chosen, left_side=True, lower=True, transpose_a=True
    )
    patterns = jnp.dot(masked, solved, precision=HIGH, preferred_element_type=jnp.float32)
    return (patterns[None], strengths)


def solution(mesh):
    split = Mesh(
        mesh.devices.reshape(mesh.shape["field"], mesh.shape["group"], 8, 4),
        ("field", "group", "row_0", "row_1"),
    )
    in_specs = (P("field", GROUP_ROW, None), P("field", GROUP_ROW), P())
    out_specs = (P("field", GROUP_ROW, None), P())
    return jax.shard_map(
        per_device, mesh=split, in_specs=in_specs, out_specs=out_specs, check_vma=False
    )
```

profile of v0, /device:TPU:1, one launch (start us, length us, event | category | flops | bytes accessed | tf_op | source)
XLA Modules:
  0.0 273.7 jit_solution(15911779829800200078)
XLA Ops:
  1.3 2.7 convolution_bitcast_fusion
  4.8 1.0 reshape_reshape.6
  5.9 16.5 %all_to_all.28 = f32[4,64,1025]{2,1,0:T(8,128)S(1)} all-to-all(f32[4,64,1025]{2,1,0:T(8,128)S(1)} %copy.15), channel_id=1, replica_groups=mesh['field'=2,'group'=8,'row_0'=8,'row_1'=4] {'row_1'}, dimensions={0} | all-to-all | bytes 2099200 | tf_op jit(solution)/shard_map/all_to_all | solution.py:20
  22.8 32.6 %all_to_all.29 = f32[64,1,1025]{2,1,0:T(1,128)S(1)} all-to-all(f32[64,1,1025]{2,1,0:T(1,128)S(1)} %all_to_all.19), channel_id=1, replica_groups=mesh['field'=2,'group'=8,'row_0'=8,'row_1'=4] {'group','row_0'}, dimensions={0} | all-to-all | bytes 524800 | tf_op jit(solution)/shard_map/all_to_all | solution.py:27
  55.7 18.1 %all_to_all.30 = f32[64,1,1025]{2,1,0:T(1,128)S(1)} all-to-all(f32[64,1,1025]{2,1,0:T(1,128)S(1)} %broadcast_in_dim.35), channel_id=1, replica_groups=mesh['field'=2,'group'=8,'row_0'=8,'row_1'=4] {'group','row_0'}, dimensions={0} | all-to-all | bytes 524800 | tf_op jit(solution)/shard_map/all_to_all | solution.py:39
  73.8 1.1 broadcast_in_dim.36
  74.9 3.7 %all-to-all-start.3 = ((f32[4,64,1025]{2,1,0:T(8,128)}), f32[4,64,1025]{2,1,0:T(8,128)S(1)}, u32[]{:S(2)}, u32[]{:S(2)}) async-start(f32[4,64,1025]{2,1,0:T(8,128)} %broadcast_in_dim.36), calls=%async_computation.3 | async-start | bytes 2359296 | tf_op jit(solution)/shard_map/all_to_all | solution.py:39
  78.7 12.1 %all-to-all-done.3 = f32[4,64,1025]{2,1,0:T(8,128)S(1)} async-done(((f32[4,64,1025]{2,1,0:T(8,128)}), f32[4,64,1025]{2,1,0:T(8,128)S(1)}, u32[]{:S(2)}, u32[]{:S(2)}) %all-to-all-start.3) | async-done | bytes 1049632 | tf_op jit(solution)/shard_map/all_to_all | solution.py:39
  94.4 11.7 %cholesky.120 = f32[128,128]{1,0:T(8,128)S(1)} custom-call(f32[128,128]{1,0:T(8,128)S(1)} %cholesky.330), custom_call_target="Cholesky" | custom-call | tf_op jit(solution)/shard_map/jit(cholesky)/cholesky | solution.py:91
  106.3 9.8 %custom-call.35 = f32[1,128,128]{1,2,0:T(8,128)S(1)} custom-call(f32[1,128,128]{2,1,0:T(8,128)S(1)} %get-tuple-element.33), custom_call_target="InvertDiagBlocksLowerTriangular" | custom-call | tf_op jit(solution)/shard_map/jit(cholesky)/cholesky | solution.py:91
  116.8 12.1 %cholesky.244 = f32[128,128]{1,0:T(8,128)S(1)} custom-call(f32[128,128]{1,0:T(8,128)S(1)} %cholesky.334), custom_call_target="Cholesky" | custom-call | tf_op jit(solution)/shard_map/jit(cholesky)/cholesky | solution.py:91
  128.9 9.8 %custom-call.36 = f32[1,128,128]{1,2,0:T(8,128)S(1)} custom-call(f32[1,128,128]{2,1,0:T(8,128)S(1)} %get-tuple-element.30), custom_call_target="InvertDiagBlocksLowerTriangular" | custom-call | tf_op jit(solution)/shard_map/jit(cholesky)/cholesky | solution.py:91
  139.4 11.7 %cholesky.265 = f32[128,128]{1,0:T(8,128)S(1)} custom-call(f32[128,128]{1,0:T(8,128)S(1)} %cholesky.339), custom_call_target="Cholesky" | custom-call | tf_op jit(solution)/shard_map/jit(cholesky)/cholesky | solution.py:91
  151.9 9.8 %custom-call.37 = f32[1,128,128]{1,2,0:T(8,128)S(1)} custom-call(f32[1,128,128]{2,1,0:T(8,128)S(1)} %get-tuple-element.27), custom_call_target="InvertDiagBlocksLowerTriangular" | custom-call | tf_op jit(solution)/shard_map/jit(cholesky)/cholesky | solution.py:91
  162.3 11.9 %cholesky.282 = f32[128,128]{1,0:T(8,128)S(1)} custom-call(f32[128,128]{1,0:T(8,128)S(1)} %convolution_subtract_fusion.2), custom_call_target="Cholesky" | custom-call | tf_op jit(solution)/shard_map/jit(cholesky)/cholesky | solution.py:91
  178.3 7.0 %collective-permute-start = (f32[512,512]{0,1:T(8,128)S(1)}, f32[512,512]{0,1:T(8,128)S(1)}, u32[]{:S(2)}, u32[]{:S(2)}) collective-permute-start(f32[512,512]{0,1:T(8,128)S(1)} %get-tuple-element.22), channel_id=1, source_target_pairs={{0,256},{256,0},{1,257},{257,1},{2,258},{258,2},{3,259},{259,3},{4... | collective-permute-start | bytes 3145736 | tf_op jit(solution)/shard_map/ppermute | solution.py:71
  185.3 10.6 %while.1 = (s32[]{:T(128)}, f32[512,512]{1,0:T(8,128)S(1)}, s32[4,2]{0,1:T(2,128)S(1)}, f32[4,128,128]{2,1,0:T(8,128)}, s32[]{:T(128)}) while((s32[]{:T(128)}, f32[512,512]{1,0:T(8,128)S(1)}, s32[4,2]{0,1:T(2,128)S(1)}, f32[4,128,128]{2,1,0:T(8,128)}, s32[]{:T(128)}) %tuple.35), condition=%wide.while_cond, body=%wide.while_body.sunk | while | flops 2 | bytes 132705 | solution.py:106
  186.0 2.0 bitcast_dynamic-update-slice_fusion.2
  188.7 2.0 bitcast_dynamic-update-slice_fusion.2
  191.3 2.0 bitcast_dynamic-update-slice_fusion.2
  193.9 2.0 bitcast_dynamic-update-slice_fusion.2
  195.9 40.2 %custom-call.38 = f32[4,128,128]{1,2,0:T(8,128)S(1)} custom-call(f32[4,128,128]{2,1,0:T(8,128)} %get-tuple-element.11), custom_call_target="InvertDiagBlocksLowerTriangular" | custom-call | tf_op jit(solution)/shard_map/triangular_solve | solution.py:106
  236.1 1.9 fusion.3
  238.0 1.1 fusion.60
  239.5 5.8 %cholesky.310 = f32[64,64]{1,0:T(8,128)S(1)} custom-call(f32[64,64]{1,0:T(8,128)S(1)} %fusion.53), custom_call_target="Cholesky" | custom-call | tf_op jit(solution)/shard_map/jit(cholesky)/cholesky | solution.py:76
  246.7 4.9 %custom-call.40 = f32[1,64,64]{1,2,0:T(8,128)S(1)} custom-call(f32[1,64,64]{2,1,0:T(8,128)S(1)} %fusion.47), custom_call_target="InvertDiagBlocksLowerTriangular" | custom-call | tf_op jit(solution)/shard_map/triangular_solve/custom-call.8 | solution.py:77
  253.1 5.8 %cholesky.321 = f32[64,64]{1,0:T(8,128)S(1)} custom-call(f32[64,64]{1,0:T(8,128)S(1)} %fusion.51), custom_call_target="Cholesky" | custom-call | tf_op jit(solution)/shard_map/jit(cholesky)/cholesky | solution.py:76
  260.3 4.9 %custom-call.41 = f32[1,64,64]{1,2,0:T(8,128)S(1)} custom-call(f32[1,64,64]{2,1,0:T(8,128)S(1)} %fusion.48), custom_call_target="InvertDiagBlocksLowerTriangular" | custom-call | tf_op jit(solution)/shard_map/triangular_solve/custom-call.8 | solution.py:77
  265.6 1.7 fusion
  268.8 1.1 convolution_subtract_fusion.4
  270.2 1.2 convolution_subtract_fusion.3
  271.7 1.9 convolution_bitcast_fusion.1
  (73 shorter events, 19.0 us)
Async XLA Ops:
  0.6 237.4 %copy-start = (f32[512,64]{0,1:T(8,128)S(1)}, f32[512,64]{0,1:T(8,128)}, u32[]{:S(2)}) copy-start(f32[512,64]{0,1:T(8,128)} %param.8) | copy-start | bytes 393220
  74.9 15.9 %all-to-all-start.3 = ((f32[4,64,1025]{2,1,0:T(8,128)}), f32[4,64,1025]{2,1,0:T(8,128)S(1)}, u32[]{:S(2)}, u32[]{:S(2)}) async-start(f32[4,64,1025]{2,1,0:T(8,128)} %broadcast_in_dim.36), calls=%async_computation.3 | async-start | bytes 2359296 | tf_op jit(solution)/shard_map/all_to_all | solution.py:39
  178.3 57.8 %collective-permute-start = (f32[512,512]{0,1:T(8,128)S(1)}, f32[512,512]{0,1:T(8,128)S(1)}, u32[]{:S(2)}, u32[]{:S(2)}) collective-permute-start(f32[512,512]{0,1:T(8,128)S(1)} %get-tuple-element.22), channel_id=1, source_target_pairs={{0,256},{256,0},{1,257},{257,1},{2,258},{258,2},{3,259},{259,3},{4... | collective-permute-start | bytes 3145736 | tf_op jit(solution)/shard_map/ppermute | solution.py:71
  195.9 40.2 %copy-start.1 = (f32[512,512]{1,0:T(8,128)}, f32[512,512]{1,0:T(8,128)S(1)}, u32[]{:S(2)}) copy-start(f32[512,512]{1,0:T(8,128)S(1)} %get-tuple-element.87) | copy-start | bytes 3145732
  265.5 6.1 %copy-start.2 = (bf16[1,1024,512]{2,1,0:T(8,128)(2,1)S(1)}, bf16[1,1024,512]{2,1,0:T(8,128)(2,1)}, u32[]{:S(2)}) copy-start(bf16[1,1024,512]{2,1,0:T(8,128)(2,1)} %param.6) | copy-start | bytes 3145732
where the time goes:
time: 278 us; the launch traced here: 274 us
  other arithmetic  145 us (52%)
  blocking collectives  67.2 us (24%)
  matrix products  17.5 us (6%)
  local copies, waits for them, and re-layouts  16.8 us (6%)
  waiting for transfers between devices  12.1 us (4%)
  starting transfers between devices  10.7 us (4%)
  between operations  4.47 us (2%)
    another operation x14, other arithmetic, per_device(): lower = jnp.linalg.cholesky(gram / count)  79 us
    another operation x2, other arithmetic, per_device(): lax.linalg.triangular_solve(lower, chosen, left_side=True, lower=True, tr...  40.2 us
    all_to_all x1, blocking collectives, summed_rows(): return jnp.sum(lax.all_to_all(own, far, 0, 0, tiled=True), axis=0)  32.6 us
    all_to_all x1, blocking collectives, copy_for_each(): return lax.all_to_all(copies, axis, split_axis=0, concat_axis=0, tiled=True)  18.1 us
    all_to_all x1, blocking collectives, sent_and_summed(): lax.all_to_all(cut_along(value, dim, devices), axis, 0, 0, tiled=True)  16.5 us
    another operation x6, other arithmetic, orthonormal(): lower = jnp.linalg.cholesky(product)  13 us
    all_to_all x1, waiting for transfers between devices, copy_for_each(): return lax.all_to_all(copies, axis, split_axis=0, concat_axis=0, tiled=True)  12.1 us
    another operation x4, other arithmetic, orthonormal(): lax.linalg.triangular_solve(lower, block, left_side=False, lower=True, tr...  11.1 us
  transfers between devices with their start and end apart: 2, of which 1 were waited for; matrix products, arithmetic and copies ran while one was open for 19% of the time, Pallas kernels for 0%

commit v1 on v0

v1 whole, which is shorter than its diff:
```python
import functools

import jax
import jax.numpy as jnp
from jax import lax
from jax.experimental import pallas as pl
from jax.experimental.pallas import tpu as pltpu
from jax.sharding import PartitionSpec as P

F32, BF16 = jnp.float32, jnp.bfloat16
NN = (((1,), (0,)), ((), ()))
NT = (((1,), (1,)), ((), ()))
TN = (((0,), (0,)), ((), ()))
MESH = pl.DeviceIdType.MESH
NX, NY, NZ = 4, 8, 8
PIECE = 5
BLOCKS = [(i, j) for i in range(4) for j in range(i, 4)]
AT = {pair: at for at, pair in enumerate(BLOCKS)}


def split(x):
    hi = x.astype(BF16)
    return hi, (x - hi.astype(F32)).astype(BF16)


def mm(a, b, dims=NN):
    ah, al = split(a)
    bh, bl = split(b)
    dot = functools.partial(lax.dot_general, dimension_numbers=dims, preferred_element_type=F32)
    return dot(ah, bh) + (dot(ah, bl) + dot(al, bh))


def across(x, k):
    return jnp.broadcast_to(x[k : k + 1, :], (8, 128))


def along(x, k):
    return jnp.broadcast_to(x[:, k : k + 1], (8, 128))


def eliminate(panel, upper, weights, leaves):
    n = panel.shape[1] // 128
    rows = 8 * leaves
    sub = lax.broadcasted_iota(jnp.int32, (8, 128), 0)
    weights[...] = jnp.zeros_like(weights)
    pivots = []
    for leaf in range(leaves):
        at = 8 * leaf
        r = [panel[at : at + 8, 128 * j : 128 * j + 128] for j in range(n)]
        c = [along(r[0], at + k) for k in range(8)]
        scale = None
        for k in range(8):
            d = across(c[k], k)
            p = 1.0 / d
            root = lax.rsqrt(d)
            pivots.append(d[0:1] * root[0:1])
            scale = p if k == 0 else jnp.where(sub >= k, p, scale)
            m = jnp.where(sub == k, 0.0, c[k] * p)
            for j in range(n):
                row = across(r[j], k)
                upper[at + k : at + k + 1, 128 * j : 128 * j + 128] = (row * root)[0:1]
                r[j] = r[j] - m * row
            for j in range(k + 1, 8):
                c[j] = c[j] - m * across(c[j], k)
        if at + 8 == rows:
            break
        for j in range(n):
            weights[at : at + 8, 128 * j : 128 * j + 128] = r[j] * scale
        if leaf:
            weights[at - 8 : at, :] = jnp.zeros((8, 128 * n), F32)
        lhs = panel[at + 8 : rows, 0:128]
        panel[at + 8 : rows, :] -= mm(lhs, weights[...])
    return pivots


def masked_rows(values, ocean):
    place = lax.broadcasted_iota(jnp.int32, (values.shape[0], 1), 0)
    return jnp.where(place < ocean, values, jnp.zeros_like(values))


def gram_kernel(ocean_ref, values_ref, out_ref):
    ocean = ocean_ref[0, 0]
    masked = masked_rows(values_ref[...], ocean)
    row = lax.broadcasted_iota(jnp.int32, (128, 128), 0)
    col = lax.broadcasted_iota(jnp.int32, (128, 128), 1)
    corner = jnp.logical_and(row == 127, col == 0)
    for i in range(4):
        product = lax.dot_general(
            masked[:, 128 * i : 128 * i + 128], masked[:, 128 * i :], TN, preferred_element_type=F32
        )
        for j in range(i, 4):
            block = product[:, 128 * (j - i) : 128 * (j - i) + 128]
            if i == j == 0:
                block = jnp.where(corner, ocean.astype(F32), block)
            out_ref[AT[i, j]] = block


def reduce_kernel(g_ref, both_ref, from_x, sum_x, from_y, sum_y, from_z, sx, rx, sy, ry, sz, rz, say, ray, sax, rax, sc, rc):
    field = lax.axis_index("field")
    y = lax.axis_index("group")
    row = lax.axis_index("row")
    z, x = row // NX, row % NX

    def at_x(other):
        return (field, y, z * NX + other)

    def at_y(other):
        return (field, other, row)

    def at_z(other):
        return (field, y, other * NX + x)

    partner = (1 - field, y, row)
    xs = [(x + d) % NX for d in range(1, NX)]
    ys = [(y + d) % NY for d in range(1, NY)]
    zs = [(z + d) % NZ for d in range(1, NZ)]
    barrier = pltpu.get_barrier_semaphore()
    everyone = [at_x(o) for o in xs] + [at_y(o) for o in ys] + [at_z(o) for o in zs] + [partner]
    for device in everyone:
        pl.semaphore_signal(barrier, inc=1, device_id=device, device_id_type=MESH)
    pl.semaphore_wait(barrier, len(everyone))

    def send(src, dst, s, r, device):
        copy = pltpu.make_async_remote_copy(
            src_ref=src, dst_ref=dst, send_sem=s, recv_sem=r, device_id=device, device_id_type=MESH
        )
        copy.start()
        return copy

    started = []
    copies = [send(g_ref.at[xs[d]], from_x.at[d], sx.at[d], rx.at[d], at_x(xs[d])) for d in range(NX - 1)]
    for copy in copies:
        copy.wait_recv()
    started += copies
    sum_x[...] = g_ref[x] + from_x[0] + from_x[1] + from_x[2]

    copies = [send(sum_x.at[ys[d]], from_y.at[d], sy.at[d], ry.at[d], at_y(ys[d])) for d in range(NY - 1)]
    for copy in copies:
        copy.wait_recv()
    started += copies
    total = sum_x[y]
    for d in range(NY - 1):
        total = total + from_y[d]
    sum_y[...] = total

    copies = [send(sum_y, from_z.at[z], sz.at[d], rz.at[d], at_z(zs[d])) for d in range(NZ - 1)]
    from_z[z] = sum_y[...]
    for copy in copies:
        copy.wait_recv()
    started += copies
    total = from_z[0]
    for other in range(1, NZ):
        total = total + from_z[other]
    mine = both_ref.at[field]
    mine[x, y] = total

    copies = [send(mine.at[x, y], mine.at[x, y], say.at[d], ray.at[d], at_y(ys[d])) for d in range(NY - 1)]
    for copy in copies:
        copy.wait_recv()
    started += copies

    copies = [send(mine.at[x], mine.at[x], sax.at[d], rax.at[d], at_x(xs[d])) for d in range(NX - 1)]
    across_chip = [send(mine.at[x], mine.at[x], sc.at[0], rc.at[0], partner)]
    for d in range(NX - 1):
        copies[d].wait_recv()
        source = (x + NX - 1 - d) % NX
        across_chip.append(send(mine.at[source], mine.at[source], sc.at[d + 1], rc.at[d + 1], partner))
    started += copies
    for copy in across_chip:
        copy.wait_recv()
    for copy in started + across_chip:
        copy.wait_send()


def all_reduced(packed):
    sems = []
    for n in (NX - 1, NY - 1, NZ - 1, NY - 1, NX - 1, NX):
        sems += [pltpu.SemaphoreType.DMA((n,))] * 2
    vm = pl.BlockSpec(memory_space=pltpu.VMEM)
    return pl.pallas_call(
        reduce_kernel,
        out_shape=jax.ShapeDtypeStruct((2, NX, NY, PIECE, 8, 128), F32),
        in_specs=[vm],
        out_specs=vm,
        scratch_shapes=[
            pltpu.VMEM((NX - 1, NY, PIECE, 8, 128), F32),
            pltpu.VMEM((NY, PIECE, 8, 128), F32),
            pltpu.VMEM((NY - 1, PIECE, 8, 128), F32),
            pltpu.VMEM((PIECE, 8, 128), F32),
            pltpu.VMEM((NZ, PIECE, 8, 128), F32),
        ]
        + sems,
        compiler_params=pltpu.CompilerParams(
            collective_id=0, has_side_effects=True, vmem_limit_bytes=32 * 2**20
        ),
    )(packed)


def modes_kernel(ocean_ref, both_ref, st_ref, values_ref, out_ref, strengths_ref, a, u, w, e, eu, st0, fin, g0, *, field):
    row = lax.broadcasted_iota(jnp.int32, (128, 128), 0)
    col = lax.broadcasted_iota(jnp.int32, (128, 128), 1)
    corner = jnp.logical_and(row == 127, col == 0)
    which = ocean_ref[0, 1] if field is None else field

    def scaled(f, at, rate):
        block = both_ref[f, at]
        if at == 0:
            block = jnp.where(corner, block[0:1, 127:128], block)
        return block * rate

    rates = []
    for f in range(2):
        rates.append(1.0 / both_ref[f, 0][127:128, 0:1])
    for i, j in BLOCKS:
        a[128 * i : 128 * i + 128, 128 * j : 128 * j + 128] = scaled(1, AT[i, j], rates[1])
        g0[AT[i, j]] = scaled(0, AT[i, j], rates[0])
    for i in range(4):
        lo, n = 128 * i, 512 - 128 * i
        at = pl.ds(lo, 128)
        eliminate(a.at[at, lo:512], u.at[at, lo:512], w.at[:, 0:n], 16)
        for j in range(i + 1, 4):
            turned = u[lo : lo + 128, 128 * j : 128 * j + 128].T
            a[128 * j : 128 * j + 128, 128 * j : 512] -= mm(turned, u[lo : lo + 128, 128 * j : 512])

    for j in range(4):
        total = None
        for i in range(j + 1):
            block = u[128 * i : 128 * i + 128, 128 * j : 128 * j + 128]
            if i == j:
                block = jnp.where(row <= col, block, 0.0)
            term = mm(st_ref[:, 128 * i : 128 * i + 128], block)
            total = term if total is None else total + term
        e[:, 128 + 128 * j : 256 + 128 * j] = total

    def times_gram(left, block):
        done = []
        for j in range(4):
            total = None
            for i in range(4):
                piece = left[:, 128 * i : 128 * i + 128]
                term = mm(piece, block(i, j)) if i <= j else mm(piece, block(j, i), NT)
                total = term if total is None else total + term
            done.append(total)
        return jnp.concatenate(done, axis=1)

    xt = e[:, 128:640]
    zt = times_gram(xt, lambda i, j: g0[AT[i, j]])
    e[:, 640:1152] = zt
    e[:, 0:128] = jnp.concatenate([mm(xt, zt, NT), jnp.zeros((64, 64), F32)], axis=1)
    eliminate(e, eu, w, 8)
    fin[0] = eu[:, 128:640]
    yt = eu[:, 640:1152]
    ft = times_gram(yt, lambda i, j: scaled(1, AT[i, j], rates[1]))
    e[:, 0:128] = jnp.concatenate([mm(ft, yt, NT), jnp.zeros((64, 64), F32)], axis=1)
    e[:, 128:640] = yt
    pivots = eliminate(e.at[:, 0:640], eu.at[:, 0:640], w.at[:, 0:640], 8)
    fin[1] = eu[:, 128:640]
    lane = lax.broadcasted_iota(jnp.int32, (1, 128), 1)
    line = jnp.zeros((1, 128), F32)
    for k, pivot in enumerate(pivots):
        line = jnp.where(lane == k, pivot, line)
    strengths_ref[...] = line
    wh, wl = split(fin[which])
    masked = masked_rows(values_ref[...], ocean_ref[0, 0])
    dot = functools.partial(lax.dot_general, dimension_numbers=NT, preferred_element_type=F32)
    out_ref[...] = dot(masked, wh) + dot(masked, wl)


def modes(info, both, st, values, field=None):
    vm = pl.BlockSpec(memory_space=pltpu.VMEM)
    return pl.pallas_call(
        functools.partial(modes_kernel, field=field),
        out_shape=(jax.ShapeDtypeStruct((1024, 64), F32), jax.ShapeDtypeStruct((1, 128), F32)),
        in_specs=[pl.BlockSpec(memory_space=pltpu.SMEM), vm, vm, vm],
        out_specs=(vm, vm),
        scratch_shapes=[
            pltpu.VMEM((512, 512), F32),
            pltpu.VMEM((512, 512), F32),
            pltpu.VMEM((128, 1152), F32),
            pltpu.VMEM((64, 1152), F32),
            pltpu.VMEM((64, 1152), F32),
            pltpu.VMEM((64, 512), F32),
            pltpu.VMEM((2, 64, 512), F32),
            pltpu.VMEM((10, 128, 128), F32),
        ],
        compiler_params=pltpu.CompilerParams(vmem_limit_bytes=48 * 2**20),
    )(info, both.reshape(2, 10, 128, 128), st, values)


def gram(info, values):
    return pl.pallas_call(
        gram_kernel,
        out_shape=jax.ShapeDtypeStruct((10, 128, 128), F32),
        in_specs=[pl.BlockSpec(memory_space=pltpu.SMEM), pl.BlockSpec(memory_space=pltpu.VMEM)],
        out_specs=pl.BlockSpec(memory_space=pltpu.VMEM),
        compiler_params=pltpu.CompilerParams(vmem_limit_bytes=32 * 2**20),
    )(info, values)


def per_device(anomalies, valid_rows, start_basis):
    values = anomalies[0]
    which = lax.axis_index("field")
    info = jnp.concatenate([valid_rows, which.astype(jnp.int32).reshape(1, 1)], axis=1)
    packed = gram(info, values)
    both = all_reduced(packed.reshape(NX, NY, PIECE, 8, 128))
    patterns, strengths = modes(info, both, start_basis.T, values)
    return patterns[None], strengths[0, :64]


def solution(mesh):
    shards = ("group", "row")
    in_specs = (P("field", shards, None), P("field", shards), P())
    out_specs = (P("field", shards, None), P())
    return jax.shard_map(
        per_device, mesh=mesh, in_specs=in_specs, out_specs=out_specs, check_vma=False
    )
```

time: 278 us -> 89.8 us (0.32); the launches traced: 274 us -> 89.7 us
  other arithmetic: 145 us -> 0.07 us
  Pallas kernels: 0 us -> 85.6 us
  blocking collectives: 67.2 us -> 0 us
  matrix products: 17.5 us -> 0 us
  local copies, waits for them, and re-layouts: 16.8 us -> 2.64 us
  waiting for transfers between devices: 12.1 us -> 0 us
  starting transfers between devices: 10.7 us -> 0 us
  between operations: 4.47 us -> 1.33 us
    another operation x26 -> x0, other arithmetic: 143 us -> none  [the longest x14 79 us: per_device(): lower = jnp.linalg.cholesky(gram / count)]
    pallas_call x0 -> x3, Pallas kernels: none -> 85.6 us  [the longest x1 52 us: all_reduced(): pl.pallas_call(reduce_kernel, out_shape=jax.ShapeDtypeStruct((2, NX, NY,...]
    all_to_all x3 -> x0, blocking collectives: 67.2 us -> none  [the longest x1 32.6 us: summed_rows(): return jnp.sum(lax.all_to_all(own, far, 0, 0, tiled=True), axis=0)]
    another operation x19 -> x0, local copies, waits for them, and re-layouts: 12.5 us -> none
    all_to_all x1 -> x0, waiting for transfers between devices: 12.1 us -> none  [copy_for_each(): return lax.all_to_all(copies, axis, split_axis=0, concat_axis=0, tiled=True)]
    dot_general x8 -> x0, matrix products: 10.7 us -> none  [the longest x2 2.89 us: per_device(): jnp.dot(coupling, right, precision=HIGH, preferred_element_type=jnp.float32)]
    ppermute x1 -> x0, starting transfers between devices: 6.99 us -> none  [from_partner(): lax.ppermute(value, axis, [(i, i ^ 1 << apart) for i in range(lax.axis_si...]
    another operation x15 -> x0, matrix products: 6.85 us -> none  [the longest x7 4.3 us: per_device(): lax.linalg.triangular_solve(lower, chosen, left_side=True, lower=True, tr...]
  transfers between devices with their start and end apart: 2 -> 0, of which waited for: 1 -> 0; matrix products, arithmetic and copies ran while one was open for 19% -> 0% of each run, Pallas kernels for 0% -> 0%
where the time goes in v1:
time: 89.8 us; the launch traced here: 89.7 us
  Pallas kernels  85.6 us (95%)
  local copies, waits for them, and re-layouts  2.64 us (3%)
  between operations  1.33 us (1%)
    pallas_call x1, Pallas kernels, all_reduced(): pl.pallas_call(reduce_kernel, out_shape=jax.ShapeDtypeStruct((2, NX, NY,...  52 us
    pallas_call x1, Pallas kernels, modes(): pl.pallas_call(functools.partial(modes_kernel, field=field), out_shape=(j...  32.4 us
    unnamed x7, local copies, waits for them, and re-layouts  2.13 us

profile of v1, /device:TPU:1, one launch (start us, length us, event | category | flops | bytes accessed | tf_op | source)
XLA Modules:
  0.0 89.7 jit_solution(11271843468074138897)
XLA Ops:
  1.3 0.1 pad_add_fusion.ocean_ref
  1.4 0.0 copy-start
  1.4 1.2 %copy-done = bf16[1,1024,512]{2,1,0:T(8,128)(2,1)S(1)} copy-done((bf16[1,1024,512]{2,1,0:T(8,128)(2,1)S(1)}, bf16[1,1024,512]{2,1,0:T(8,128)(2,1)}, u32[]{:S(2)}) %copy-start) | copy-done | bytes 1048600
  2.6 1.2 %shard_map.50 = f32[10,128,128]{2,1,0:T(8,128)S(1)} custom-call(s32[1,2]{1,0:T(1,128)S(1)} %pad_add_fusion.ocean_ref, bf16[1024,512]{1,0:T(8,128)(2,1)S(1)} %bitcast.9), custom_call_target="tpu_custom_call" | custom-call | tf_op jit(solution)/shard_map/pallas_call | solution.py:291
  3.8 0.0 copy-start.1
  3.8 0.0 copy-start.2
  3.8 52.0 %shard_map.51 = f32[2,4,8,5,8,128]{5,4,3,2,1,0:T(8,128)S(1)} custom-call(f32[4,8,5,8,128]{4,3,2,1,0:T(8,128)S(1)} %bitcast.11), custom_call_target="tpu_custom_call" | custom-call | tf_op jit(solution)/shard_map/pallas_call | solution.py:180
  55.8 0.0 copy-done.1
  55.9 0.0 copy-done.2
  55.9 32.4 %shard_map.52 = (f32[1024,64]{1,0:T(8,128)S(1)}, f32[1,128]{1,0:T(1,128)S(1)}) custom-call(s32[1,2]{1,0:T(1,128)S(1)} %pad_add_fusion.ocean_ref, f32[2,10,128,128]{3,2,1,0:T(8,128)S(1)} %bitcast.8, f32[64,512]{1,0:T(8,128)S(1)} %bitcast.13, bf16[1024,512]{1,0:T(8,128)(2,1)S(1)} %bitcast.10), custom_call_target="tpu_custom_call" | custom-call | tf_op jit(solution)/shard_map/pallas_call | solution.py:271
  88.3 0.9 copy.5
  89.2 0.5 slice_bitcast_fusion
Async XLA Ops:
  1.4 1.2 %copy-start = (bf16[1,1024,512]{2,1,0:T(8,128)(2,1)S(1)}, bf16[1,1024,512]{2,1,0:T(8,128)(2,1)}, u32[]{:S(2)}) copy-start(bf16[1,1024,512]{2,1,0:T(8,128)(2,1)} %param.3) | copy-start | bytes 3145732
  3.8 52.1 %copy-start.1 = (bf16[1,1024,512]{2,1,0:T(8,128)(2,1)S(1)}, bf16[1,1024,512]{2,1,0:T(8,128)(2,1)}, u32[]{:S(2)}) copy-start(bf16[1,1024,512]{2,1,0:T(8,128)(2,1)} %param.3) | copy-start | bytes 3145732
  3.8 52.1 %copy-start.2 = (f32[512,64]{0,1:T(8,128)S(1)}, f32[512,64]{0,1:T(8,128)}, u32[]{:S(2)}) copy-start(f32[512,64]{0,1:T(8,128)} %param.5) | copy-start | bytes 393220

commit v2 on v1

--- a/solution.py
+++ b/solution.py
@@ -14,6 +14,7 @@
 MESH = pl.DeviceIdType.MESH
 NX, NY, NZ = 4, 8, 8
 PIECE = 5
+TALL = 16
 BLOCKS = [(i, j) for i in range(4) for j in range(i, 4)]
 AT = {pair: at for at, pair in enumerate(BLOCKS)}
 
@@ -38,38 +39,49 @@
     return jnp.broadcast_to(x[:, k : k + 1], (8, 128))
 
 
-def eliminate(panel, upper, weights, leaves):
+def eliminate(panel, upper, weights, rows):
     n = panel.shape[1] // 128
-    rows = 8 * leaves
     sub = lax.broadcasted_iota(jnp.int32, (8, 128), 0)
     weights[...] = jnp.zeros_like(weights)
     pivots = []
-    for leaf in range(leaves):
-        at = 8 * leaf
-        r = [panel[at : at + 8, 128 * j : 128 * j + 128] for j in range(n)]
-        c = [along(r[0], at + k) for k in range(8)]
-        scale = None
-        for k in range(8):
-            d = across(c[k], k)
+    for at in range(0, rows, TALL):
+        r = [
+            [panel[at + 8 * v : at + 8 * v + 8, 128 * j : 128 * j + 128] for j in range(n)]
+            for v in range(TALL // 8)
+        ]
+        c = [[along(r[v][0], at + k) for k in range(TALL)] for v in range(TALL // 8)]
+        scale = [None] * len(r)
+        kept = [[None] * n for _ in r]
+        for k in range(TALL):
+            o, s = divmod(k, 8)
+            d = across(c[o][k], s)
             p = 1.0 / d
             root = lax.rsqrt(d)
             pivots.append(d[0:1] * root[0:1])
-            scale = p if k == 0 else jnp.where(sub >= k, p, scale)
-            m = jnp.where(sub == k, 0.0, c[k] * p)
+            scale[o] = p if s == 0 else jnp.where(sub >= s, p, scale[o])
+            m = [c[v][k] * p for v in range(len(r))]
+            m[o] = jnp.where(sub == s, 0.0, m[o])
             for j in range(n):
-                row = across(r[j], k)
-                upper[at + k : at + k + 1, 128 * j : 128 * j + 128] = (row * root)[0:1]
-                r[j] = r[j] - m * row
-            for j in range(k + 1, 8):
-                c[j] = c[j] - m * across(c[j], k)
-        if at + 8 == rows:
+                row = across(r[o][j], s)
+                now = r[o][j] * root
+                kept[o][j] = now if s == 0 else jnp.where(sub >= s, now, kept[o][j])
+                for v in range(len(r)):
+                    r[v][j] = r[v][j] - m[v] * row
+            for q in range(k + 1, TALL):
+                row = across(c[o][q], s)
+                for v in range(len(r)):
+                    c[v][q] = c[v][q] - m[v] * row
+        for v in range(len(r)):
+            for j in range(n):
+                upper[at + 8 * v : at + 8 * v + 8, 128 * j : 128 * j + 128] = kept[v][j]
+        if at + TALL == rows:
             break
-        for j in range(n):
-            weights[at : at + 8, 128 * j : 128 * j + 128] = r[j] * scale
-        if leaf:
-            weights[at - 8 : at, :] = jnp.zeros((8, 128 * n), F32)
-        lhs = panel[at + 8 : rows, 0:128]
-        panel[at + 8 : rows, :] -= mm(lhs, weights[...])
+        for v in range(len(r)):
+            for j in range(n):
+                weights[at + 8 * v : at + 8 * v + 8, 128 * j : 128 * j + 128] = r[v][j] * scale[v]
+        if at:
+            weights[at - TALL : at, :] = jnp.zeros((TALL, 128 * n), F32)
+        panel[at + TALL : rows, :] -= mm(panel[at + TALL : rows, 0:128], weights[...])
     return pivots
 
 
@@ -78,9 +90,8 @@
     return jnp.where(place < ocean, values, jnp.zeros_like(values))
 
 
-def gram_kernel(ocean_ref, values_ref, out_ref):
-    ocean = ocean_ref[0, 0]
-    masked = masked_rows(values_ref[...], ocean)
+def put_gram(ocean, values, out_ref):
+    masked = masked_rows(values, ocean)
     row = lax.broadcasted_iota(jnp.int32, (128, 128), 0)
     col = lax.broadcasted_iota(jnp.int32, (128, 128), 1)
     corner = jnp.logical_and(row == 127, col == 0)
@@ -92,10 +103,13 @@
             block = product[:, 128 * (j - i) : 128 * (j - i) + 128]
             if i == j == 0:
                 block = jnp.where(corner, ocean.astype(F32), block)
-            out_ref[AT[i, j]] = block
-
-
-def reduce_kernel(g_ref, both_ref, from_x, sum_x, from_y, sum_y, from_z, sx, rx, sy, ry, sz, rz, say, ray, sax, rax, sc, rc):
+            at = 16 * AT[i, j]
+            for t in range(16):
+                tile = at + t
+                out_ref[tile // 40, tile % 40 // PIECE, tile % PIECE] = block[8 * t : 8 * t + 8, :]
+
+
+def reduce_kernel(ocean_ref, values_hbm, both_ref, values, g_ref, sv, from_x, sum_x, from_y, sum_y, from_z, sx, rx, sy, ry, sz, rz, say, ray, sax, rax, sc, rc):
     field = lax.axis_index("field")
     y = lax.axis_index("group")
     row = lax.axis_index("row")
@@ -118,6 +132,10 @@
     everyone = [at_x(o) for o in xs] + [at_y(o) for o in ys] + [at_z(o) for o in zs] + [partner]
     for device in everyone:
         pl.semaphore_signal(barrier, inc=1, device_id=device, device_id_type=MESH)
+    load = pltpu.make_async_copy(values_hbm, values, sv)
+    load.start()
+    load.wait()
+    put_gram(ocean_ref[0, 0], values[...], g_ref)
     pl.semaphore_wait(barrier, len(everyone))
 
     def send(src, dst, s, r, device):
@@ -172,7 +190,7 @@
         copy.wait_send()
 
 
-def all_reduced(packed):
+def all_reduced(ocean, values):
     sems = []
     for n in (NX - 1, NY - 1, NZ - 1, NY - 1, NX - 1, NX):
         sems += [pltpu.SemaphoreType.DMA((n,))] * 2
@@ -180,9 +198,12 @@
     return pl.pallas_call(
         reduce_kernel,
         out_shape=jax.ShapeDtypeStruct((2, NX, NY, PIECE, 8, 128), F32),
-        in_specs=[vm],
+        in_specs=[pl.BlockSpec(memory_space=pltpu.SMEM), pl.BlockSpec(memory_space=pltpu.HBM)],
         out_specs=vm,
         scratch_shapes=[
+            pltpu.VMEM((1024, 512), BF16),
+            pltpu.VMEM((NX, NY, PIECE, 8, 128), F32),
+            pltpu.SemaphoreType.DMA,
             pltpu.VMEM((NX - 1, NY, PIECE, 8, 128), F32),
             pltpu.VMEM((NY, PIECE, 8, 128), F32),
             pltpu.VMEM((NY - 1, PIECE, 8, 128), F32),
@@ -193,14 +214,14 @@
         compiler_params=pltpu.CompilerParams(
             collective_id=0, has_side_effects=True, vmem_limit_bytes=32 * 2**20
         ),
-    )(packed)
-
-
-def modes_kernel(ocean_ref, both_ref, st_ref, values_ref, out_ref, strengths_ref, a, u, w, e, eu, st0, fin, g0, *, field):
+    )(ocean, values)
+
+
+def modes_kernel(ocean_ref, both_ref, st_ref, values_ref, out_ref, strengths_ref, a, u, w, e, eu, st0, fin, g0):
     row = lax.broadcasted_iota(jnp.int32, (128, 128), 0)
     col = lax.broadcasted_iota(jnp.int32, (128, 128), 1)
     corner = jnp.logical_and(row == 127, col == 0)
-    which = ocean_ref[0, 1] if field is None else field
+    which = lax.axis_index("field")
 
     def scaled(f, at, rate):
         block = both_ref[f, at]
@@ -217,7 +238,7 @@
     for i in range(4):
         lo, n = 128 * i, 512 - 128 * i
         at = pl.ds(lo, 128)
-        eliminate(a.at[at, lo:512], u.at[at, lo:512], w.at[:, 0:n], 16)
+        eliminate(a.at[at, lo:512], u.at[at, lo:512], w.at[:, 0:n], 128)
         for j in range(i + 1, 4):
             turned = u[lo : lo + 128, 128 * j : 128 * j + 128].T
             a[128 * j : 128 * j + 128, 128 * j : 512] -= mm(turned, u[lo : lo + 128, 128 * j : 512])
@@ -247,30 +268,30 @@
     zt = times_gram(xt, lambda i, j: g0[AT[i, j]])
     e[:, 640:1152] = zt
     e[:, 0:128] = jnp.concatenate([mm(xt, zt, NT), jnp.zeros((64, 64), F32)], axis=1)
-    eliminate(e, eu, w, 8)
+    eliminate(e, eu, w, 64)
     fin[0] = eu[:, 128:640]
     yt = eu[:, 640:1152]
     ft = times_gram(yt, lambda i, j: scaled(1, AT[i, j], rates[1]))
     e[:, 0:128] = jnp.concatenate([mm(ft, yt, NT), jnp.zeros((64, 64), F32)], axis=1)
     e[:, 128:640] = yt
-    pivots = eliminate(e.at[:, 0:640], eu.at[:, 0:640], w.at[:, 0:640], 8)
+    pivots = eliminate(e.at[:, 0:640], eu.at[:, 0:640], w.at[:, 0:640], 64)
     fin[1] = eu[:, 128:640]
     lane = lax.broadcasted_iota(jnp.int32, (1, 128), 1)
     line = jnp.zeros((1, 128), F32)
     for k, pivot in enumerate(pivots):
         line = jnp.where(lane == k, pivot, line)
-    strengths_ref[...] = line
+    strengths_ref[...] = line[:, 0:64]
     wh, wl = split(fin[which])
     masked = masked_rows(values_ref[...], ocean_ref[0, 0])
-    dot = functools.partial(lax.dot_general, dimension_numbers=NT, preferred_element_type=F32)
-    out_ref[...] = dot(masked, wh) + dot(masked, wl)
-
-
-def modes(info, both, st, values, field=None):
+    halves = lax.dot_general(jnp.concatenate([wh, wl], axis=0), masked, NT, preferred_element_type=F32)
+    out_ref[...] = halves[0:64] + halves[64:128]
+
+
+def modes(ocean, both, st, values):
     vm = pl.BlockSpec(memory_space=pltpu.VMEM)
     return pl.pallas_call(
-        functools.partial(modes_kernel, field=field),
-        out_shape=(jax.ShapeDtypeStruct((1024, 64), F32), jax.ShapeDtypeStruct((1, 128), F32)),
+        modes_kernel,
+        out_shape=(jax.ShapeDtypeStruct((64, 1024), F32), jax.ShapeDtypeStruct((1, 64), F32)),
         in_specs=[pl.BlockSpec(memory_space=pltpu.SMEM), vm, vm, vm],
         out_specs=(vm, vm),
         scratch_shapes=[
@@ -284,27 +305,14 @@
             pltpu.VMEM((10, 128, 128), F32),
         ],
         compiler_params=pltpu.CompilerParams(vmem_limit_bytes=48 * 2**20),
-    )(info, both.reshape(2, 10, 128, 128), st, values)
-
-
-def gram(info, values):
-    return pl.pallas_call(
-        gram_kernel,
-        out_shape=jax.ShapeDtypeStruct((10, 128, 128), F32),
-        in_specs=[pl.BlockSpec(memory_space=pltpu.SMEM), pl.BlockSpec(memory_space=pltpu.VMEM)],
-        out_specs=pl.BlockSpec(memory_space=pltpu.VMEM),
-        compiler_params=pltpu.CompilerParams(vmem_limit_bytes=32 * 2**20),
-    )(info, values)
+    )(ocean, both.reshape(2, 10, 128, 128), st, values)
 
 
 def per_device(anomalies, valid_rows, start_basis):
     values = anomalies[0]
-    which = lax.axis_index("field")
-    info = jnp.concatenate([valid_rows, which.astype(jnp.int32).reshape(1, 1)], axis=1)
-    packed = gram(info, values)
-    both = all_reduced(packed.reshape(NX, NY, PIECE, 8, 128))
-    patterns, strengths = modes(info, both, start_basis.T, values)
-    return patterns[None], strengths[0, :64]
+    both = all_reduced(valid_rows, values)
+    patterns, strengths = modes(valid_rows, both, start_basis.T, values)
+    return patterns.T[None], strengths.reshape(64)
 
 
 def solution(mesh):

time: 89.8 us -> 76.2 us (0.85)
  Pallas kernels: 85.6 us -> 73.5 us
  local copies, waits for them, and re-layouts: 2.64 us -> 1.23 us
    pallas_call x2 -> x1, Pallas kernels: 33.6 us -> 21.5 us  [modes(): pl.pallas_call(modes_kernel, out_shape=(jax.ShapeDtypeStruct((64, 1024),...]
    unnamed x7 -> x6, local copies, waits for them, and re-layouts: 2.13 us -> 1.23 us
where the time goes in v2:
time: 76.2 us; the launch traced here: 76.1 us
  Pallas kernels  73.5 us (96%)
  between operations  1.31 us (2%)
  local copies, waits for them, and re-layouts  1.23 us (2%)
    pallas_call x1, Pallas kernels, all_reduced(): pl.pallas_call(reduce_kernel, out_shape=jax.ShapeDtypeStruct((2, NX, NY,...  52.1 us
    pallas_call x1, Pallas kernels, modes(): pl.pallas_call(modes_kernel, out_shape=(jax.ShapeDtypeStruct((64, 1024),...  21.5 us

profile of v2, /device:TPU:1, one launch (start us, length us, event | category | flops | bytes accessed | tf_op | source)
XLA Modules:
  0.0 76.1 jit_solution(16014342077853442214)
XLA Ops:
  1.3 0.0 copy-start
  1.3 1.2 %copy-done = bf16[1,1024,512]{2,1,0:T(8,128)(2,1)S(1)} copy-done((bf16[1,1024,512]{2,1,0:T(8,128)(2,1)S(1)}, bf16[1,1024,512]{2,1,0:T(8,128)(2,1)}, u32[]{:S(2)}) %copy-start) | copy-done | bytes 1048600
  2.5 0.0 copy-start.1
  2.5 0.0 copy-start.2
  2.5 52.1 %shard_map.50 = f32[2,4,8,5,8,128]{5,4,3,2,1,0:T(8,128)S(1)} custom-call(s32[1,1]{1,0:T(1,128)S(6)} %copy.5.ocean_ref, bf16[1024,512]{1,0:T(8,128)(2,1)S(1)} %bitcast.8), custom_call_target="tpu_custom_call" | custom-call | tf_op jit(solution)/shard_map/pallas_call | solution.py:198
  54.6 0.0 copy-done.1
  54.6 0.0 copy-done.2
  54.6 21.5 %shard_map.51 = (f32[64,1024]{1,0:T(8,128)}, f32[1,64]{1,0:T(1,128)}) custom-call(s32[1,1]{1,0:T(1,128)S(6)} %copy.5.ocean_ref, f32[2,10,128,128]{3,2,1,0:T(8,128)S(1)} %bitcast.7, f32[64,512]{1,0:T(8,128)S(1)} %bitcast.10, bf16[1024,512]{1,0:T(8,128)(2,1)S(1)} %bitcast.9), custom_call_target="tpu_custom_call" | custom-call | tf_op jit(solution)/shard_map/pallas_call | solution.py:292
Async XLA Ops:
  1.3 1.2 %copy-start = (bf16[1,1024,512]{2,1,0:T(8,128)(2,1)S(1)}, bf16[1,1024,512]{2,1,0:T(8,128)(2,1)}, u32[]{:S(2)}) copy-start(bf16[1,1024,512]{2,1,0:T(8,128)(2,1)} %param.3) | copy-start | bytes 3145732
  2.5 52.1 %copy-start.1 = (bf16[1,1024,512]{2,1,0:T(8,128)(2,1)S(1)}, bf16[1,1024,512]{2,1,0:T(8,128)(2,1)}, u32[]{:S(2)}) copy-start(bf16[1,1024,512]{2,1,0:T(8,128)(2,1)} %param.3) | copy-start | bytes 3145732
  2.5 52.1 %copy-start.2 = (f32[512,64]{0,1:T(8,128)S(1)}, f32[512,64]{0,1:T(8,128)}, u32[]{:S(2)}) copy-start(f32[512,64]{0,1:T(8,128)} %param.5) | copy-start | bytes 393220

commit v3 on v2

--- a/solution.py
+++ b/solution.py
@@ -12,8 +12,10 @@
 NT = (((1,), (1,)), ((), ()))
 TN = (((0,), (0,)), ((), ()))
 MESH = pl.DeviceIdType.MESH
-NX, NY, NZ = 4, 8, 8
-PIECE = 5
+NX = 4
+SIZE = {"x": NX, "y": 8, "z": 8}
+FAR = {4: (1, 3, 2), 8: (1, 7, 2, 6, 3, 5, 4)}
+STREAMS = (("x", "y", "z", 64), ("y", "x", "z", 32), ("z", "x", "y", 64))
 TALL = 16
 BLOCKS = [(i, j) for i in range(4) for j in range(i, 4)]
 AT = {pair: at for at, pair in enumerate(BLOCKS)}
@@ -103,114 +105,169 @@
             block = product[:, 128 * (j - i) : 128 * (j - i) + 128]
             if i == j == 0:
                 block = jnp.where(corner, ocean.astype(F32), block)
-            at = 16 * AT[i, j]
-            for t in range(16):
-                tile = at + t
-                out_ref[tile // 40, tile % 40 // PIECE, tile % PIECE] = block[8 * t : 8 * t + 8, :]
-
-
-def reduce_kernel(ocean_ref, values_hbm, both_ref, values, g_ref, sv, from_x, sum_x, from_y, sum_y, from_z, sx, rx, sy, ry, sz, rz, say, ray, sax, rax, sc, rc):
+            out_ref[16 * AT[i, j] : 16 * AT[i, j] + 16] = block.reshape(16, 8, 128)
+
+
+class Stream:
+    SCRATCH = 17
+
+    def __init__(self, spec, start, refs, me, device, partner, own, mine):
+        self.a, self.b, self.c, tiles = spec
+        self.na, self.nb, self.nc = SIZE[self.a], SIZE[self.b], SIZE[self.c]
+        self.unit = tiles // (self.na * self.nb)
+        self.start = start
+        self.from_a, self.sum_a, self.from_b, self.sum_b, self.from_c = refs[:5]
+        self.sems = refs[5:]
+        self.me, self.device, self.partner = me, device, partner
+        self.own, self.mine = own, mine
+        self.started, self.live, self.over = [], [], []
+
+    @staticmethod
+    def scratch(spec):
+        a, b, c, tiles = spec
+        na, nb, nc = SIZE[a], SIZE[b], SIZE[c]
+        unit = tiles // (na * nb)
+        shapes = [(na - 1, nb * unit), (nb * unit,), (nb - 1, unit), (unit,), (nc, unit)]
+        sems = []
+        for n in (na - 1, nb - 1, nc - 1, nb - 1, na - 1, na):
+            sems += [pltpu.SemaphoreType.DMA((n,))] * 2
+        return [pltpu.VMEM((*shape, 8, 128), F32) for shape in shapes] + sems
+
+    def part(self, i):
+        return pl.ds(self.start + i * (self.nb * self.unit), self.nb * self.unit)
+
+    def piece(self, i, j):
+        return pl.ds(self.start + (i * self.nb + j) * self.unit, self.unit)
+
+    def send(self, phase, k, src, dst, device):
+        copy = pltpu.make_async_remote_copy(
+            src_ref=src,
+            dst_ref=dst,
+            send_sem=self.sems[2 * phase].at[k],
+            recv_sem=self.sems[2 * phase + 1].at[k],
+            device_id=device,
+            device_id_type=MESH,
+        )
+        copy.start()
+        self.started.append(copy)
+        return copy
+
+    def to_all(self, phase, axis, src, dst):
+        size = SIZE[axis]
+        self.live = []
+        for k, far in enumerate(FAR[size]):
+            other = (self.me[axis] + far) % size
+            self.live.append(self.send(phase, k, src(other), dst(k), self.device[axis](other)))
+
+    def received(self):
+        for copy in self.live:
+            copy.wait_recv()
+
+    def scatter_a(self):
+        self.to_all(0, self.a, lambda o: self.own.at[self.part(o)], lambda k: self.from_a.at[k])
+
+    def scatter_b(self):
+        self.received()
+        total = self.own[self.part(self.me[self.a])]
+        for k in range(self.na - 1):
+            total = total + self.from_a[k]
+        self.sum_a[...] = total
+        unit = self.unit
+        self.to_all(
+            1, self.b, lambda o: self.sum_a.at[pl.ds(o * unit, unit)], lambda k: self.from_b.at[k]
+        )
+
+    def exchange_c(self):
+        self.received()
+        total = self.sum_a[pl.ds(self.me[self.b] * self.unit, self.unit)]
+        for k in range(self.nb - 1):
+            total = total + self.from_b[k]
+        self.sum_b[...] = total
+        place = self.me[self.c]
+        self.to_all(2, self.c, lambda o: self.sum_b, lambda k: self.from_c.at[place])
+        self.from_c[place] = total
+
+    def gather_b(self):
+        self.received()
+        total = self.from_c[0]
+        for k in range(1, self.nc):
+            total = total + self.from_c[k]
+        at = self.piece(self.me[self.a], self.me[self.b])
+        self.mine[at] = total
+        self.to_all(3, self.b, lambda o: self.mine.at[at], lambda k: self.mine.at[at])
+
+    def gather_a(self):
+        self.received()
+        at = self.part(self.me[self.a])
+        self.to_all(4, self.a, lambda o: self.mine.at[at], lambda k: self.mine.at[at])
+        self.over = [self.send(5, 0, self.mine.at[at], self.mine.at[at], self.partner)]
+
+    def hand_over(self):
+        gathered = self.live
+        for k, far in enumerate(FAR[self.na]):
+            gathered[k].wait_recv()
+            at = self.part((self.me[self.a] + self.na - far) % self.na)
+            self.over.append(self.send(5, k + 1, self.mine.at[at], self.mine.at[at], self.partner))
+
+    def close(self):
+        for copy in self.over:
+            copy.wait_recv()
+        for copy in self.started:
+            copy.wait_send()
+
+
+STEPS = ("scatter_a", "scatter_b", "exchange_c", "gather_b", "gather_a", "hand_over", "close")
+
+
+def reduce_kernel(ocean_ref, values_hbm, both_ref, values, own, loaded, *refs):
     field = lax.axis_index("field")
     y = lax.axis_index("group")
     row = lax.axis_index("row")
     z, x = row // NX, row % NX
-
-    def at_x(other):
-        return (field, y, z * NX + other)
-
-    def at_y(other):
-        return (field, other, row)
-
-    def at_z(other):
-        return (field, y, other * NX + x)
-
+    me = {"x": x, "y": y, "z": z}
+    device = {
+        "x": lambda other: (field, y, z * NX + other),
+        "y": lambda other: (field, other, row),
+        "z": lambda other: (field, y, other * NX + x),
+    }
     partner = (1 - field, y, row)
-    xs = [(x + d) % NX for d in range(1, NX)]
-    ys = [(y + d) % NY for d in range(1, NY)]
-    zs = [(z + d) % NZ for d in range(1, NZ)]
     barrier = pltpu.get_barrier_semaphore()
-    everyone = [at_x(o) for o in xs] + [at_y(o) for o in ys] + [at_z(o) for o in zs] + [partner]
-    for device in everyone:
-        pl.semaphore_signal(barrier, inc=1, device_id=device, device_id_type=MESH)
-    load = pltpu.make_async_copy(values_hbm, values, sv)
+    everyone = [partner]
+    for axis, size in SIZE.items():
+        everyone += [device[axis]((me[axis] + far) % size) for far in FAR[size]]
+    for other in everyone:
+        pl.semaphore_signal(barrier, inc=1, device_id=other, device_id_type=MESH)
+    load = pltpu.make_async_copy(values_hbm, values, loaded)
     load.start()
     load.wait()
-    put_gram(ocean_ref[0, 0], values[...], g_ref)
+    put_gram(ocean_ref[0, 0], values[...], own)
     pl.semaphore_wait(barrier, len(everyone))
 
-    def send(src, dst, s, r, device):
-        copy = pltpu.make_async_remote_copy(
-            src_ref=src, dst_ref=dst, send_sem=s, recv_sem=r, device_id=device, device_id_type=MESH
-        )
-        copy.start()
-        return copy
-
-    started = []
-    copies = [send(g_ref.at[xs[d]], from_x.at[d], sx.at[d], rx.at[d], at_x(xs[d])) for d in range(NX - 1)]
-    for copy in copies:
-        copy.wait_recv()
-    started += copies
-    sum_x[...] = g_ref[x] + from_x[0] + from_x[1] + from_x[2]
-
-    copies = [send(sum_x.at[ys[d]], from_y.at[d], sy.at[d], ry.at[d], at_y(ys[d])) for d in range(NY - 1)]
-    for copy in copies:
-        copy.wait_recv()
-    started += copies
-    total = sum_x[y]
-    for d in range(NY - 1):
-        total = total + from_y[d]
-    sum_y[...] = total
-
-    copies = [send(sum_y, from_z.at[z], sz.at[d], rz.at[d], at_z(zs[d])) for d in range(NZ - 1)]
-    from_z[z] = sum_y[...]
-    for copy in copies:
-        copy.wait_recv()
-    started += copies
-    total = from_z[0]
-    for other in range(1, NZ):
-        total = total + from_z[other]
-    mine = both_ref.at[field]
-    mine[x, y] = total
-
-    copies = [send(mine.at[x, y], mine.at[x, y], say.at[d], ray.at[d], at_y(ys[d])) for d in range(NY - 1)]
-    for copy in copies:
-        copy.wait_recv()
-    started += copies
-
-    copies = [send(mine.at[x], mine.at[x], sax.at[d], rax.at[d], at_x(xs[d])) for d in range(NX - 1)]
-    across_chip = [send(mine.at[x], mine.at[x], sc.at[0], rc.at[0], partner)]
-    for d in range(NX - 1):
-        copies[d].wait_recv()
-        source = (x + NX - 1 - d) % NX
-        across_chip.append(send(mine.at[source], mine.at[source], sc.at[d + 1], rc.at[d + 1], partner))
-    started += copies
-    for copy in across_chip:
-        copy.wait_recv()
-    for copy in started + across_chip:
-        copy.wait_send()
+    streams, start = [], 0
+    for k, spec in enumerate(STREAMS):
+        mine = refs[Stream.SCRATCH * k : Stream.SCRATCH * (k + 1)]
+        streams.append(Stream(spec, start, mine, me, device, partner, own, both_ref.at[field]))
+        start += spec[3]
+    for step in STEPS:
+        for stream in streams:
+            getattr(stream, step)()
 
 
 def all_reduced(ocean, values):
-    sems = []
-    for n in (NX - 1, NY - 1, NZ - 1, NY - 1, NX - 1, NX):
-        sems += [pltpu.SemaphoreType.DMA((n,))] * 2
-    vm = pl.BlockSpec(memory_space=pltpu.VMEM)
+    scratch = []
+    for spec in STREAMS:
+        scratch += Stream.scratch(spec)
     return pl.pallas_call(
         reduce_kernel,
-        out_shape=jax.ShapeDtypeStruct((2, NX, NY, PIECE, 8, 128), F32),
+        out_shape=jax.ShapeDtypeStruct((2, 160, 8, 128), F32),
         in_specs=[pl.BlockSpec(memory_space=pltpu.SMEM), pl.BlockSpec(memory_space=pltpu.HBM)],
-        out_specs=vm,
+        out_specs=pl.BlockSpec(memory_space=pltpu.VMEM),
         scratch_shapes=[
             pltpu.VMEM((1024, 512), BF16),
-            pltpu.VMEM((NX, NY, PIECE, 8, 128), F32),
+            pltpu.VMEM((160, 8, 128), F32),
             pltpu.SemaphoreType.DMA,
-            pltpu.VMEM((NX - 1, NY, PIECE, 8, 128), F32),
-            pltpu.VMEM((NY, PIECE, 8, 128), F32),
-            pltpu.VMEM((NY - 1, PIECE, 8, 128), F32),
-            pltpu.VMEM((PIECE, 8, 128), F32),
-            pltpu.VMEM((NZ, PIECE, 8, 128), F32),
         ]
-        + sems,
+        + scratch,
         compiler_params=pltpu.CompilerParams(
             collective_id=0, has_side_effects=True, vmem_limit_bytes=32 * 2**20
         ),

time: 76.2 us -> 70.5 us (0.925)
  Pallas kernels: 73.5 us -> 67.8 us
    pallas_call x1, Pallas kernels: 52.1 us -> 46.1 us  [all_reduced(): pl.pallas_call(reduce_kernel, out_shape=jax.ShapeDtypeStruct((2, 160, 8,...]
where the time goes in v3:
time: 70.5 us; the launch traced here: 70.3 us
  Pallas kernels  67.8 us (96%)
  between operations  1.31 us (2%)
  local copies, waits for them, and re-layouts  1.23 us (2%)
    pallas_call x1, Pallas kernels, all_reduced(): pl.pallas_call(reduce_kernel, out_shape=jax.ShapeDtypeStruct((2, 160, 8,...  46.1 us
    pallas_call x1, Pallas kernels, modes(): pl.pallas_call(modes_kernel, out_shape=(jax.ShapeDtypeStruct((64, 1024),...  21.7 us

profile of v3, /device:TPU:1, one launch (start us, length us, event | category | flops | bytes accessed | tf_op | source)
XLA Modules:
  0.0 70.3 jit_solution(9865232467030498032)
XLA Ops:
  1.3 0.0 copy-start
  1.3 1.2 %copy-done = bf16[1,1024,512]{2,1,0:T(8,128)(2,1)S(1)} copy-done((bf16[1,1024,512]{2,1,0:T(8,128)(2,1)S(1)}, bf16[1,1024,512]{2,1,0:T(8,128)(2,1)}, u32[]{:S(2)}) %copy-start) | copy-done | bytes 1048600
  2.5 0.0 copy-start.1
  2.5 0.0 copy-start.2
  2.5 46.1 %shard_map.50 = f32[2,160,8,128]{3,2,1,0:T(8,128)S(1)} custom-call(s32[1,1]{1,0:T(1,128)S(6)} %copy.5.ocean_ref, bf16[1024,512]{1,0:T(8,128)(2,1)S(1)} %bitcast.8), custom_call_target="tpu_custom_call" | custom-call | tf_op jit(solution)/shard_map/pallas_call | solution.py:260
  48.6 0.0 copy-done.1
  48.7 0.0 copy-done.2
  48.7 21.7 %shard_map.51 = (f32[64,1024]{1,0:T(8,128)}, f32[1,64]{1,0:T(1,128)}) custom-call(s32[1,1]{1,0:T(1,128)S(6)} %copy.5.ocean_ref, f32[2,10,128,128]{3,2,1,0:T(8,128)S(1)} %bitcast.7, f32[64,512]{1,0:T(8,128)S(1)} %bitcast.10, bf16[1024,512]{1,0:T(8,128)(2,1)S(1)} %bitcast.9), custom_call_target="tpu_custom_call" | custom-call | tf_op jit(solution)/shard_map/pallas_call | solution.py:349
Async XLA Ops:
  1.3 1.2 %copy-start = (bf16[1,1024,512]{2,1,0:T(8,128)(2,1)S(1)}, bf16[1,1024,512]{2,1,0:T(8,128)(2,1)}, u32[]{:S(2)}) copy-start(bf16[1,1024,512]{2,1,0:T(8,128)(2,1)} %param.3) | copy-start | bytes 3145732
  2.5 46.1 %copy-start.1 = (bf16[1,1024,512]{2,1,0:T(8,128)(2,1)S(1)}, bf16[1,1024,512]{2,1,0:T(8,128)(2,1)}, u32[]{:S(2)}) copy-start(bf16[1,1024,512]{2,1,0:T(8,128)(2,1)} %param.3) | copy-start | bytes 3145732
  2.5 46.2 %copy-start.2 = (f32[512,64]{0,1:T(8,128)S(1)}, f32[512,64]{0,1:T(8,128)}, u32[]{:S(2)}) copy-start(f32[512,64]{0,1:T(8,128)} %param.5) | copy-start | bytes 393220

commit v4 on v3

--- a/solution.py
+++ b/solution.py
@@ -120,7 +120,7 @@
         self.sems = refs[5:]
         self.me, self.device, self.partner = me, device, partner
         self.own, self.mine = own, mine
-        self.started, self.live, self.over = [], [], []
+        self.started, self.live = [], []
 
     @staticmethod
     def scratch(spec):
@@ -200,26 +200,59 @@
         self.received()
         at = self.part(self.me[self.a])
         self.to_all(4, self.a, lambda o: self.mine.at[at], lambda k: self.mine.at[at])
-        self.over = [self.send(5, 0, self.mine.at[at], self.mine.at[at], self.partner)]
+
+    def over(self, k):
+        far = (0, *FAR[self.na])[k]
+        at = self.part((self.me[self.a] + self.na - far) % self.na)
+        return pltpu.make_async_remote_copy(
+            src_ref=self.mine.at[at],
+            dst_ref=self.mine.at[at],
+            send_sem=self.sems[10].at[k],
+            recv_sem=self.sems[11].at[k],
+            device_id=self.partner,
+            device_id_type=MESH,
+        )
 
     def hand_over(self):
-        gathered = self.live
-        for k, far in enumerate(FAR[self.na]):
-            gathered[k].wait_recv()
+        for k in range(self.na):
+            if k:
+                self.live[k - 1].wait_recv()
+            self.over(k).start()
+
+    def taken_over(self, theirs):
+        for k in range(self.na):
+            far = (0, *FAR[self.na])[k]
             at = self.part((self.me[self.a] + self.na - far) % self.na)
-            self.over.append(self.send(5, k + 1, self.mine.at[at], self.mine.at[at], self.partner))
-
-    def close(self):
-        for copy in self.over:
-            copy.wait_recv()
-        for copy in self.started:
-            copy.wait_send()
-
-
-STEPS = ("scatter_a", "scatter_b", "exchange_c", "gather_b", "gather_a", "hand_over", "close")
-
-
-def reduce_kernel(ocean_ref, values_hbm, both_ref, values, own, loaded, *refs):
+            pltpu.make_async_remote_copy(
+                src_ref=theirs.at[at],
+                dst_ref=theirs.at[at],
+                send_sem=self.sems[10].at[k],
+                recv_sem=self.sems[11].at[k],
+                device_id=self.partner,
+                device_id_type=MESH,
+            ).wait_recv()
+
+
+def times_gram(left, block):
+    done = []
+    for j in range(4):
+        total = None
+        for i in range(4):
+            piece = left[:, 128 * i : 128 * i + 128]
+            term = mm(piece, block(i, j)) if i <= j else mm(piece, block(j, i), NT)
+            total = term if total is None else total + term
+        done.append(total)
+    return jnp.concatenate(done, axis=1)
+
+
+def square(product):
+    return jnp.concatenate([product, jnp.zeros_like(product)], axis=1)
+
+
+def whole_kernel(
+    ocean_ref, st_ref, values_hbm, out_ref, strengths_ref,
+    values, own, both, a, u, w, e, eu, fin, xt, line, loaded, go, sx, rx, sl, rl, *refs
+):
     field = lax.axis_index("field")
     y = lax.axis_index("group")
     row = lax.axis_index("row")
@@ -231,6 +264,7 @@
         "z": lambda other: (field, y, other * NX + x),
     }
     partner = (1 - field, y, row)
+    first, second = field == 0, field == 1
     barrier = pltpu.get_barrier_semaphore()
     everyone = [partner]
     for axis, size in SIZE.items():
@@ -246,129 +280,177 @@
     streams, start = [], 0
     for k, spec in enumerate(STREAMS):
         mine = refs[Stream.SCRATCH * k : Stream.SCRATCH * (k + 1)]
-        streams.append(Stream(spec, start, mine, me, device, partner, own, both_ref.at[field]))
+        streams.append(Stream(spec, start, mine, me, device, partner, own, both.at[field]))
         start += spec[3]
-    for step in STEPS:
+
+    @pl.when(first)
+    def _():
+        pl.semaphore_wait(go, 1)
+
+    for stream in streams:
+        stream.scatter_a()
+    for stream in streams:
+        stream.scatter_b()
+
+    @pl.when(second)
+    def _():
+        pl.semaphore_signal(go, inc=1, device_id=partner, device_id_type=MESH)
+
+    for step in ("exchange_c", "gather_b", "gather_a"):
         for stream in streams:
             getattr(stream, step)()
 
-
-def all_reduced(ocean, values):
+    line_row = lax.broadcasted_iota(jnp.int32, (128, 128), 0)
+    line_col = lax.broadcasted_iota(jnp.int32, (128, 128), 1)
+    corner = jnp.logical_and(line_row == 127, line_col == 0)
+
+    def raw(f, at):
+        return both[f, 16 * at : 16 * at + 16].reshape(128, 128)
+
+    def scaled(f, at, rate):
+        block = raw(f, at)
+        if at == 0:
+            block = jnp.where(corner, block[0:1, 127:128], block)
+        return block * rate
+
+    def rate_of(f):
+        return 1.0 / raw(f, 0)[127:128, 0:1]
+
+    def across_chip(j):
+        return pltpu.make_async_remote_copy(
+            src_ref=xt.at[j], dst_ref=xt.at[j], send_sem=sx.at[j], recv_sem=rx.at[j],
+            device_id=partner, device_id_type=MESH,
+        )
+
+    def strengths_across():
+        return pltpu.make_async_remote_copy(
+            src_ref=line, dst_ref=line, send_sem=sl, recv_sem=rl,
+            device_id=partner, device_id_type=MESH,
+        )
+
+    @pl.when(first)
+    def _():
+        for stream in streams:
+            stream.hand_over()
+        for j in range(4):
+            across_chip(j).wait_recv()
+
+    @pl.when(second)
+    def _():
+        for stream in streams:
+            stream.received()
+        rate = rate_of(1)
+        for i, j in BLOCKS:
+            a[128 * i : 128 * i + 128, 128 * j : 128 * j + 128] = scaled(1, AT[i, j], rate)
+        for i in range(4):
+            lo, n = 128 * i, 512 - 128 * i
+            at = pl.ds(lo, 128)
+            eliminate(a.at[at, lo:512], u.at[at, lo:512], w.at[:, 0:n], 128)
+            for j in range(i + 1, 4):
+                turned = u[lo : lo + 128, 128 * j : 128 * j + 128].T
+                a[128 * j : 128 * j + 128, 128 * j : 512] -= mm(turned, u[lo : lo + 128, 128 * j : 512])
+            total = None
+            for k in range(i + 1):
+                block = u[128 * k : 128 * k + 128, lo : lo + 128]
+                if k == i:
+                    block = jnp.where(line_row <= line_col, block, 0.0)
+                term = mm(st_ref[:, 128 * k : 128 * k + 128], block)
+                total = term if total is None else total + term
+            xt[i] = total
+            across_chip(i).start()
+        for stream in streams:
+            stream.taken_over(both.at[0])
+
+    rate0 = rate_of(0)
+    left = jnp.concatenate([xt[j] for j in range(4)], axis=1)
+    zt = times_gram(left, lambda i, j: scaled(0, AT[i, j], rate0))
+    e[:, 128:640] = left
+    e[:, 640:1152] = zt
+    e[:, 0:128] = square(mm(left, zt, NT))
+    eliminate(e, eu, w, 64)
+
+    @pl.when(first)
+    def _():
+        fin[...] = eu[:, 128:640]
+
+    @pl.when(second)
+    def _():
+        rate1 = rate_of(1)
+        yt = eu[:, 640:1152]
+        ft = times_gram(yt, lambda i, j: scaled(1, AT[i, j], rate1))
+        e[:, 0:128] = square(mm(ft, yt, NT))
+        e[:, 128:640] = yt
+        pivots = eliminate(e.at[:, 0:640], eu.at[:, 0:640], w.at[:, 0:640], 64)
+        fin[...] = eu[:, 128:640]
+        lane = lax.broadcasted_iota(jnp.int32, (8, 128), 1)
+        drawn = jnp.zeros((8, 128), F32)
+        for k, pivot in enumerate(pivots):
+            drawn = jnp.where(lane == k, pivot, drawn)
+        line[...] = drawn
+        strengths_across().start()
+
+    wh, wl = split(fin[...])
+    masked = masked_rows(values[...], ocean_ref[0, 0])
+    halves = lax.dot_general(jnp.concatenate([wh, wl], axis=0), masked, NT, preferred_element_type=F32)
+    out_ref[...] = halves[0:64] + halves[64:128]
+
+    @pl.when(first)
+    def _():
+        strengths_across().wait_recv()
+        for stream in streams:
+            for k in range(stream.na):
+                stream.over(k).wait_send()
+
+    @pl.when(second)
+    def _():
+        strengths_across().wait_send()
+        for j in range(4):
+            across_chip(j).wait_send()
+
+    for stream in streams:
+        for copy in stream.started:
+            copy.wait_send()
+    strengths_ref[...] = line[0:1, 0:64]
+
+
+def whole(ocean, st, values):
     scratch = []
     for spec in STREAMS:
         scratch += Stream.scratch(spec)
+    vm = pl.BlockSpec(memory_space=pltpu.VMEM)
     return pl.pallas_call(
-        reduce_kernel,
-        out_shape=jax.ShapeDtypeStruct((2, 160, 8, 128), F32),
-        in_specs=[pl.BlockSpec(memory_space=pltpu.SMEM), pl.BlockSpec(memory_space=pltpu.HBM)],
-        out_specs=pl.BlockSpec(memory_space=pltpu.VMEM),
+        whole_kernel,
+        out_shape=(jax.ShapeDtypeStruct((64, 1024), F32), jax.ShapeDtypeStruct((1, 64), F32)),
+        in_specs=[pl.BlockSpec(memory_space=pltpu.SMEM), vm, pl.BlockSpec(memory_space=pltpu.HBM)],
+        out_specs=(vm, vm),
         scratch_shapes=[
             pltpu.VMEM((1024, 512), BF16),
             pltpu.VMEM((160, 8, 128), F32),
-            pltpu.SemaphoreType.DMA,
-        ]
-        + scratch,
-        compiler_params=pltpu.CompilerParams(
-            collective_id=0, has_side_effects=True, vmem_limit_bytes=32 * 2**20
-        ),
-    )(ocean, values)
-
-
-def modes_kernel(ocean_ref, both_ref, st_ref, values_ref, out_ref, strengths_ref, a, u, w, e, eu, st0, fin, g0):
-    row = lax.broadcasted_iota(jnp.int32, (128, 128), 0)
-    col = lax.broadcasted_iota(jnp.int32, (128, 128), 1)
-    corner = jnp.logical_and(row == 127, col == 0)
-    which = lax.axis_index("field")
-
-    def scaled(f, at, rate):
-        block = both_ref[f, at]
-        if at == 0:
-            block = jnp.where(corner, block[0:1, 127:128], block)
-        return block * rate
-
-    rates = []
-    for f in range(2):
-        rates.append(1.0 / both_ref[f, 0][127:128, 0:1])
-    for i, j in BLOCKS:
-        a[128 * i : 128 * i + 128, 128 * j : 128 * j + 128] = scaled(1, AT[i, j], rates[1])
-        g0[AT[i, j]] = scaled(0, AT[i, j], rates[0])
-    for i in range(4):
-        lo, n = 128 * i, 512 - 128 * i
-        at = pl.ds(lo, 128)
-        eliminate(a.at[at, lo:512], u.at[at, lo:512], w.at[:, 0:n], 128)
-        for j in range(i + 1, 4):
-            turned = u[lo : lo + 128, 128 * j : 128 * j + 128].T
-            a[128 * j : 128 * j + 128, 128 * j : 512] -= mm(turned, u[lo : lo + 128, 128 * j : 512])
-
-    for j in range(4):
-        total = None
-        for i in range(j + 1):
-            block = u[128 * i : 128 * i + 128, 128 * j : 128 * j + 128]
-            if i == j:
-                block = jnp.where(row <= col, block, 0.0)
-            term = mm(st_ref[:, 128 * i : 128 * i + 128], block)
-            total = term if total is None else total + term
-        e[:, 128 + 128 * j : 256 + 128 * j] = total
-
-    def times_gram(left, block):
-        done = []
-        for j in range(4):
-            total = None
-            for i in range(4):
-                piece = left[:, 128 * i : 128 * i + 128]
-                term = mm(piece, block(i, j)) if i <= j else mm(piece, block(j, i), NT)
-                total = term if total is None else total + term
-            done.append(total)
-        return jnp.concatenate(done, axis=1)
-
-    xt = e[:, 128:640]
-    zt = times_gram(xt, lambda i, j: g0[AT[i, j]])
-    e[:, 640:1152] = zt
-    e[:, 0:128] = jnp.concatenate([mm(xt, zt, NT), jnp.zeros((64, 64), F32)], axis=1)
-    eliminate(e, eu, w, 64)
-    fin[0] = eu[:, 128:640]
-    yt = eu[:, 640:1152]
-    ft = times_gram(yt, lambda i, j: scaled(1, AT[i, j], rates[1]))
-    e[:, 0:128] = jnp.concatenate([mm(ft, yt, NT), jnp.zeros((64, 64), F32)], axis=1)
-    e[:, 128:640] = yt
-    pivots = eliminate(e.at[:, 0:640], eu.at[:, 0:640], w.at[:, 0:640], 64)
-    fin[1] = eu[:, 128:640]
-    lane = lax.broadcasted_iota(jnp.int32, (1, 128), 1)
-    line = jnp.zeros((1, 128), F32)
-    for k, pivot in enumerate(pivots):
-        line = jnp.where(lane == k, pivot, line)
-    strengths_ref[...] = line[:, 0:64]
-    wh, wl = split(fin[which])
-    masked = masked_rows(values_ref[...], ocean_ref[0, 0])
-    halves = lax.dot_general(jnp.concatenate([wh, wl], axis=0), masked, NT, preferred_element_type=F32)
-    out_ref[...] = halves[0:64] + halves[64:128]
-
-
-def modes(ocean, both, st, values):
-    vm = pl.BlockSpec(memory_space=pltpu.VMEM)
-    return pl.pallas_call(
-        modes_kernel,
-        out_shape=(jax.ShapeDtypeStruct((64, 1024), F32), jax.ShapeDtypeStruct((1, 64), F32)),
-        in_specs=[pl.BlockSpec(memory_space=pltpu.SMEM), vm, vm, vm],
-        out_specs=(vm, vm),
-        scratch_shapes=[
+            pltpu.VMEM((2, 160, 8, 128), F32),
             pltpu.VMEM((512, 512), F32),
             pltpu.VMEM((512, 512), F32),
             pltpu.VMEM((128, 1152), F32),
             pltpu.VMEM((64, 1152), F32),
             pltpu.VMEM((64, 1152), F32),
             pltpu.VMEM((64, 512), F32),
-            pltpu.VMEM((2, 64, 512), F32),
-            pltpu.VMEM((10, 128, 128), F32),
-        ],
-        compiler_params=pltpu.CompilerParams(vmem_limit_bytes=48 * 2**20),
-    )(ocean, both.reshape(2, 10, 128, 128), st, values)
+            pltpu.VMEM((4, 64, 128), F32),
+            pltpu.VMEM((8, 128), F32),
+            pltpu.SemaphoreType.DMA,
+            pltpu.SemaphoreType.REGULAR,
+            pltpu.SemaphoreType.DMA((4,)),
+            pltpu.SemaphoreType.DMA((4,)),
+            pltpu.SemaphoreType.DMA,
+            pltpu.SemaphoreType.DMA,
+        ]
+        + scratch,
+        compiler_params=pltpu.CompilerParams(
+            collective_id=0, has_side_effects=True, vmem_limit_bytes=60 * 2**20
+        ),
+    )(ocean, st, values)
 
 
 def per_device(anomalies, valid_rows, start_basis):
-    values = anomalies[0]
-    both = all_reduced(valid_rows, values)
-    patterns, strengths = modes(valid_rows, both, start_basis.T, values)
+    patterns, strengths = whole(valid_rows, start_basis.T, anomalies[0])
     return patterns.T[None], strengths.reshape(64)
 
 

time: 70.5 us -> 68.6 us (0.973)
  Pallas kernels: 67.8 us -> 64.9 us
  local copies, waits for them, and re-layouts: 1.23 us -> 2.19 us
    pallas_call x2 -> x1, Pallas kernels: 67.8 us -> 64.9 us  [whole(): pl.pallas_call(whole_kernel, out_shape=(jax.ShapeDtypeStruct((64, 1024),...]
    unnamed x6 -> x4, local copies, waits for them, and re-layouts: 1.23 us -> 2.19 us
where the time goes in v4:
time: 68.6 us; the launch traced here: 68.4 us
  Pallas kernels  64.9 us (95%)
  local copies, waits for them, and re-layouts  2.19 us (3%)
  between operations  1.29 us (2%)
    pallas_call x1, Pallas kernels, whole(): pl.pallas_call(whole_kernel, out_shape=(jax.ShapeDtypeStruct((64, 1024),...  64.9 us
    unnamed x4, local copies, waits for them, and re-layouts  2.19 us

profile of v4, /device:TPU:1, one launch (start us, length us, event | category | flops | bytes accessed | tf_op | source)
XLA Modules:
  0.0 68.4 jit_solution(7999752747566044963)
XLA Ops:
  1.3 64.9 %shard_map.50 = (f32[64,1024]{1,0:T(8,128)}, f32[1,64]{1,0:T(1,128)}) custom-call(s32[1,1]{1,0:T(1,128)S(6)} %copy.7.ocean_ref, f32[64,512]{1,0:T(8,128)} %bitcast.8, bf16[1024,512]{1,0:T(8,128)(2,1)} %bitcast.6), custom_call_target="tpu_custom_call" | custom-call | tf_op jit(solution)/shard_map/pallas_call | solution.py:421
  66.2 0.0 copy-start
  66.2 1.7 %copy.8 = f32[1,1024,64]{1,2,0:T(8,128)} copy(f32[1,1024,64]{1,2,0:T(8,128)} %bitcast.7) | data formatting | bytes 524288
  67.9 0.0 copy-done
  67.9 0.5 copy.9
Async XLA Ops:
  66.2 1.7 %copy-start = (f32[1,64]{1,0:T(1,128)S(1)}, f32[1,64]{1,0:T(1,128)}, u32[]{:S(2)}) copy-start(f32[1,64]{1,0:T(1,128)} %get-tuple-element.5) | copy-start | bytes 772

commit v5 on v4

--- a/solution.py
+++ b/solution.py
@@ -15,7 +15,7 @@
 NX = 4
 SIZE = {"x": NX, "y": 8, "z": 8}
 FAR = {4: (1, 3, 2), 8: (1, 7, 2, 6, 3, 5, 4)}
-STREAMS = (("x", "y", "z", 64), ("y", "x", "z", 32), ("z", "x", "y", 64))
+STREAMS = (("x", "y", "z", 64), ("z", "x", "y", 32), ("x", "z", "y", 64))
 TALL = 16
 BLOCKS = [(i, j) for i in range(4) for j in range(i, 4)]
 AT = {pair: at for at, pair in enumerate(BLOCKS)}
@@ -92,8 +92,7 @@
     return jnp.where(place < ocean, values, jnp.zeros_like(values))
 
 
-def put_gram(ocean, values, out_ref):
-    masked = masked_rows(values, ocean)
+def put_gram(ocean, masked, out_ref):
     row = lax.broadcasted_iota(jnp.int32, (128, 128), 0)
     col = lax.broadcasted_iota(jnp.int32, (128, 128), 1)
     corner = jnp.logical_and(row == 127, col == 0)
@@ -250,8 +249,8 @@
 
 
 def whole_kernel(
-    ocean_ref, st_ref, values_hbm, out_ref, strengths_ref,
-    values, own, both, a, u, w, e, eu, fin, xt, line, loaded, go, sx, rx, sl, rl, *refs
+    ocean_ref, st_hbm, values_hbm, masked, fin, line,
+    own, both, a, u, w, e, eu, xt, st_ref, loaded, brought, go, sx, rx, sl, rl, *refs
 ):
     field = lax.axis_index("field")
     y = lax.axis_index("group")
@@ -271,10 +270,14 @@
         everyone += [device[axis]((me[axis] + far) % size) for far in FAR[size]]
     for other in everyone:
         pl.semaphore_signal(barrier, inc=1, device_id=other, device_id_type=MESH)
-    load = pltpu.make_async_copy(values_hbm, values, loaded)
+    load = pltpu.make_async_copy(values_hbm, masked, loaded)
     load.start()
+    bring = pltpu.make_async_copy(st_hbm, st_ref, brought)
+    bring.start()
     load.wait()
-    put_gram(ocean_ref[0, 0], values[...], own)
+    bring.wait()
+    masked[...] = masked_rows(masked[...], ocean_ref[0, 0])
+    put_gram(ocean_ref[0, 0], masked, own)
     pl.semaphore_wait(barrier, len(everyone))
 
     streams, start = [], 0
@@ -283,22 +286,21 @@
         streams.append(Stream(spec, start, mine, me, device, partner, own, both.at[field]))
         start += spec[3]
 
-    @pl.when(first)
-    def _():
-        pl.semaphore_wait(go, 1)
-
     for stream in streams:
         stream.scatter_a()
     for stream in streams:
         stream.scatter_b()
 
-    @pl.when(second)
-    def _():
-        pl.semaphore_signal(go, inc=1, device_id=partner, device_id_type=MESH)
-
-    for step in ("exchange_c", "gather_b", "gather_a"):
+    for step in ("exchange_c", "gather_b"):
         for stream in streams:
             getattr(stream, step)()
+
+    @pl.when(first)
+    def _():
+        pl.semaphore_wait(go, 1)
+
+    for stream in streams:
+        stream.gather_a()
 
     line_row = lax.broadcasted_iota(jnp.int32, (128, 128), 0)
     line_col = lax.broadcasted_iota(jnp.int32, (128, 128), 1)
@@ -339,6 +341,7 @@
     def _():
         for stream in streams:
             stream.received()
+        pl.semaphore_signal(go, inc=1, device_id=partner, device_id_type=MESH)
         rate = rate_of(1)
         for i, j in BLOCKS:
             a[128 * i : 128 * i + 128, 128 * j : 128 * j + 128] = scaled(1, AT[i, j], rate)
@@ -364,10 +367,9 @@
     rate0 = rate_of(0)
     left = jnp.concatenate([xt[j] for j in range(4)], axis=1)
     zt = times_gram(left, lambda i, j: scaled(0, AT[i, j], rate0))
-    e[:, 128:640] = left
-    e[:, 640:1152] = zt
+    e[:, 128:640] = jnp.where(first, left, zt)
     e[:, 0:128] = square(mm(left, zt, NT))
-    eliminate(e, eu, w, 64)
+    eliminate(e, eu, w.at[:, 0:640], 64)
 
     @pl.when(first)
     def _():
@@ -376,11 +378,11 @@
     @pl.when(second)
     def _():
         rate1 = rate_of(1)
-        yt = eu[:, 640:1152]
+        yt = eu[:, 128:640]
         ft = times_gram(yt, lambda i, j: scaled(1, AT[i, j], rate1))
         e[:, 0:128] = square(mm(ft, yt, NT))
         e[:, 128:640] = yt
-        pivots = eliminate(e.at[:, 0:640], eu.at[:, 0:640], w.at[:, 0:640], 64)
+        pivots = eliminate(e, eu, w.at[:, 0:640], 64)
         fin[...] = eu[:, 128:640]
         lane = lax.broadcasted_iota(jnp.int32, (8, 128), 1)
         drawn = jnp.zeros((8, 128), F32)
@@ -389,11 +391,6 @@
         line[...] = drawn
         strengths_across().start()
 
-    wh, wl = split(fin[...])
-    masked = masked_rows(values[...], ocean_ref[0, 0])
-    halves = lax.dot_general(jnp.concatenate([wh, wl], axis=0), masked, NT, preferred_element_type=F32)
-    out_ref[...] = halves[0:64] + halves[64:128]
-
     @pl.when(first)
     def _():
         strengths_across().wait_recv()
@@ -410,7 +407,6 @@
     for stream in streams:
         for copy in stream.started:
             copy.wait_send()
-    strengths_ref[...] = line[0:1, 0:64]
 
 
 def whole(ocean, st, values):
@@ -420,21 +416,24 @@
     vm = pl.BlockSpec(memory_space=pltpu.VMEM)
     return pl.pallas_call(
         whole_kernel,
-        out_shape=(jax.ShapeDtypeStruct((64, 1024), F32), jax.ShapeDtypeStruct((1, 64), F32)),
-        in_specs=[pl.BlockSpec(memory_space=pltpu.SMEM), vm, pl.BlockSpec(memory_space=pltpu.HBM)],
-        out_specs=(vm, vm),
+        out_shape=(
+            jax.ShapeDtypeStruct((1024, 512), BF16),
+            jax.ShapeDtypeStruct((64, 512), F32),
+            jax.ShapeDtypeStruct((8, 128), F32),
+        ),
+        in_specs=[pl.BlockSpec(memory_space=pltpu.SMEM)] + [pl.BlockSpec(memory_space=pltpu.HBM)] * 2,
+        out_specs=(vm, vm, vm),
         scratch_shapes=[
-            pltpu.VMEM((1024, 512), BF16),
             pltpu.VMEM((160, 8, 128), F32),
             pltpu.VMEM((2, 160, 8, 128), F32),
             pltpu.VMEM((512, 512), F32),
             pltpu.VMEM((512, 512), F32),
-            pltpu.VMEM((128, 1152), F32),
-            pltpu.VMEM((64, 1152), F32),
-            pltpu.VMEM((64, 1152), F32),
+            pltpu.VMEM((128, 640), F32),
+            pltpu.VMEM((64, 640), F32),
+            pltpu.VMEM((64, 640), F32),
+            pltpu.VMEM((4, 64, 128), F32),
             pltpu.VMEM((64, 512), F32),
-            pltpu.VMEM((4, 64, 128), F32),
-            pltpu.VMEM((8, 128), F32),
+            pltpu.SemaphoreType.DMA,
             pltpu.SemaphoreType.DMA,
             pltpu.SemaphoreType.REGULAR,
             pltpu.SemaphoreType.DMA((4,)),
@@ -444,13 +443,34 @@
         ]
         + scratch,
         compiler_params=pltpu.CompilerParams(
-            collective_id=0, has_side_effects=True, vmem_limit_bytes=60 * 2**20
+            collective_id=0, has_side_effects=True, vmem_limit_bytes=419 * 2**17
         ),
     )(ocean, st, values)
 
 
+def patterns_kernel(masked_ref, fin_ref, line_ref, out_ref, strengths_ref):
+    wh, wl = split(fin_ref[...])
+    halves = lax.dot_general(
+        jnp.concatenate([wh, wl], axis=0), masked_ref[...], NT, preferred_element_type=F32
+    )
+    out_ref[...] = halves[0:64] + halves[64:128]
+    strengths_ref[...] = line_ref[0:1, 0:64]
+
+
+def patterns_of(masked, fin, line):
+    vm = pl.BlockSpec(memory_space=pltpu.VMEM)
+    return pl.pallas_call(
+        patterns_kernel,
+        out_shape=(jax.ShapeDtypeStruct((64, 1024), F32), jax.ShapeDtypeStruct((1, 64), F32)),
+        in_specs=[vm] * 3,
+        out_specs=(vm, vm),
+        compiler_params=pltpu.CompilerParams(vmem_limit_bytes=32 * 2**20),
+    )(masked, fin, line)
+
+
 def per_device(anomalies, valid_rows, start_basis):
-    patterns, strengths = whole(valid_rows, start_basis.T, anomalies[0])
+    kept = whole(valid_rows, start_basis.T, anomalies[0])
+    patterns, strengths = patterns_of(*kept)
     return patterns.T[None], strengths.reshape(64)
 
 

time: 68.6 us -> 65.8 us (0.959)
  Pallas kernels: 64.9 us -> 63.4 us
  local copies, waits for them, and re-layouts: 2.19 us -> 0.9 us
    pallas_call x1 -> x2, Pallas kernels: 64.9 us -> 63.4 us  [the longest x1 62.3 us: whole(): pl.pallas_call(whole_kernel, out_shape=(jax.ShapeDtypeStruct((1024, 512),...]
    unnamed x4 -> x2, local copies, waits for them, and re-layouts: 2.19 us -> 0.9 us
where the time goes in v5:
time: 65.8 us; the launch traced here: 65.6 us
  Pallas kernels  63.4 us (96%)
  between operations  1.29 us (2%)
  local copies, waits for them, and re-layouts  0.9 us (1%)
    pallas_call x1, Pallas kernels, whole(): pl.pallas_call(whole_kernel, out_shape=(jax.ShapeDtypeStruct((1024, 512),...  62.3 us

profile of v5, /device:TPU:1, one launch (start us, length us, event | category | flops | bytes accessed | tf_op | source)
XLA Modules:
  0.0 65.6 jit_solution(5488378648523494046)
XLA Ops:
  1.3 0.0 copy-start
  1.3 0.9 %copy-done = f32[512,64]{0,1:T(8,128)S(1)} copy-done((f32[512,64]{0,1:T(8,128)S(1)}, f32[512,64]{0,1:T(8,128)}, u32[]{:S(2)}) %copy-start) | copy-done | bytes 131096
  2.2 62.3 %shard_map.50 = (bf16[1024,512]{1,0:T(8,128)(2,1)S(1)}, f32[64,512]{1,0:T(8,128)S(1)}, f32[8,128]{1,0:T(8,128)S(1)}) custom-call(s32[1,1]{1,0:T(1,128)S(6)} %copy.5.ocean_ref, f32[64,512]{1,0:T(8,128)S(1)} %bitcast.6, bf16[1024,512]{1,0:T(8,128)(2,1)} %bitcast.7), custom_call_target="tpu_custom_call" | custom-call | tf_op jit(solution)/shard_map/pallas_call | solution.py:417
  64.5 1.2 %shard_map.51 = (f32[64,1024]{1,0:T(8,128)}, f32[1,64]{1,0:T(1,128)}) custom-call(bf16[1024,512]{1,0:T(8,128)(2,1)S(1)} %get-tuple-element.7.masked_ref, f32[64,512]{1,0:T(8,128)S(1)} %get-tuple-element.8.fin_ref, f32[8,128]{1,0:T(8,128)S(1)} %get-tuple-element.9.line_ref), custom_call_target="tpu_custom_call" | custom-call | tf_op jit(solution)/shard_map/pallas_call | solution.py:462
Async XLA Ops:
  1.3 0.9 %copy-start = (f32[512,64]{0,1:T(8,128)S(1)}, f32[512,64]{0,1:T(8,128)}, u32[]{:S(2)}) copy-start(f32[512,64]{0,1:T(8,128)} %param.5) | copy-start | bytes 393220

commit v6 on v5

--- a/solution.py
+++ b/solution.py
@@ -92,11 +92,11 @@
     return jnp.where(place < ocean, values, jnp.zeros_like(values))
 
 
-def put_gram(ocean, masked, out_ref):
+def put_gram(ocean, masked, out_ref, block_rows):
     row = lax.broadcasted_iota(jnp.int32, (128, 128), 0)
     col = lax.broadcasted_iota(jnp.int32, (128, 128), 1)
     corner = jnp.logical_and(row == 127, col == 0)
-    for i in range(4):
+    for i in block_rows:
         product = lax.dot_general(
             masked[:, 128 * i : 128 * i + 128], masked[:, 128 * i :], TN, preferred_element_type=F32
         )
@@ -277,7 +277,7 @@
     load.wait()
     bring.wait()
     masked[...] = masked_rows(masked[...], ocean_ref[0, 0])
-    put_gram(ocean_ref[0, 0], masked, own)
+    put_gram(ocean_ref[0, 0], masked, own, (0,))
     pl.semaphore_wait(barrier, len(everyone))
 
     streams, start = [], 0
@@ -286,7 +286,9 @@
         streams.append(Stream(spec, start, mine, me, device, partner, own, both.at[field]))
         start += spec[3]
 
-    for stream in streams:
+    streams[0].scatter_a()
+    put_gram(ocean_ref[0, 0], masked, own, (1, 2, 3))
+    for stream in streams[1:]:
         stream.scatter_a()
     for stream in streams:
         stream.scatter_b()
@@ -339,17 +341,26 @@
 
     @pl.when(second)
     def _():
-        for stream in streams:
-            stream.received()
+        streams[0].received()
         pl.semaphore_signal(go, inc=1, device_id=partner, device_id_type=MESH)
         rate = rate_of(1)
-        for i, j in BLOCKS:
-            a[128 * i : 128 * i + 128, 128 * j : 128 * j + 128] = scaled(1, AT[i, j], rate)
         for i in range(4):
+            if i == 1:
+                for stream in streams[1:]:
+                    stream.received()
+                for k, j in BLOCKS:
+                    if k:
+                        later = scaled(1, AT[k, j], rate)
+                        turned = u[0:128, 128 * k : 128 * k + 128].T
+                        later = later - mm(turned, u[0:128, 128 * j : 128 * j + 128])
+                        a[128 * k : 128 * k + 128, 128 * j : 128 * j + 128] = later
+            elif i == 0:
+                for j in range(4):
+                    a[0:128, 128 * j : 128 * j + 128] = scaled(1, AT[0, j], rate)
             lo, n = 128 * i, 512 - 128 * i
             at = pl.ds(lo, 128)
             eliminate(a.at[at, lo:512], u.at[at, lo:512], w.at[:, 0:n], 128)
-            for j in range(i + 1, 4):
+            for j in range(i + 1, 4) if i else ():
                 turned = u[lo : lo + 128, 128 * j : 128 * j + 128].T
                 a[128 * j : 128 * j + 128, 128 * j : 512] -= mm(turned, u[lo : lo + 128, 128 * j : 512])
             total = None

time: 65.8 us -> 63.5 us (0.965)
  Pallas kernels: 63.4 us -> 61.1 us
    pallas_call x1, Pallas kernels: 62.3 us -> 59.9 us  [whole(): pl.pallas_call(whole_kernel, out_shape=(jax.ShapeDtypeStruct((1024, 512),...]
where the time goes in v6:
time: 63.5 us; the launch traced here: 63.3 us
  Pallas kernels  61.1 us (96%)
  between operations  1.29 us (2%)
  local copies, waits for them, and re-layouts  0.9 us (1%)
    pallas_call x1, Pallas kernels, whole(): pl.pallas_call(whole_kernel, out_shape=(jax.ShapeDtypeStruct((1024, 512),...  59.9 us

profile of v6, /device:TPU:1, one launch (start us, length us, event | category | flops | bytes accessed | tf_op | source)
XLA Modules:
  0.0 63.3 jit_solution(9271366701032601284)
XLA Ops:
  1.3 0.0 copy-start
  1.3 0.9 %copy-done = f32[512,64]{0,1:T(8,128)S(1)} copy-done((f32[512,64]{0,1:T(8,128)S(1)}, f32[512,64]{0,1:T(8,128)}, u32[]{:S(2)}) %copy-start) | copy-done | bytes 131096
  2.2 59.9 %shard_map.50 = (bf16[1024,512]{1,0:T(8,128)(2,1)S(1)}, f32[64,512]{1,0:T(8,128)S(1)}, f32[8,128]{1,0:T(8,128)S(1)}) custom-call(s32[1,1]{1,0:T(1,128)S(6)} %copy.5.ocean_ref, f32[64,512]{1,0:T(8,128)S(1)} %bitcast.6, bf16[1024,512]{1,0:T(8,128)(2,1)} %bitcast.7), custom_call_target="tpu_custom_call" | custom-call | tf_op jit(solution)/shard_map/pallas_call | solution.py:428
  62.1 1.2 %shard_map.51 = (f32[64,1024]{1,0:T(8,128)}, f32[1,64]{1,0:T(1,128)}) custom-call(bf16[1024,512]{1,0:T(8,128)(2,1)S(1)} %get-tuple-element.7.masked_ref, f32[64,512]{1,0:T(8,128)S(1)} %get-tuple-element.8.fin_ref, f32[8,128]{1,0:T(8,128)S(1)} %get-tuple-element.9.line_ref), custom_call_target="tpu_custom_call" | custom-call | tf_op jit(solution)/shard_map/pallas_call | solution.py:473
Async XLA Ops:
  1.3 0.9 %copy-start = (f32[512,64]{0,1:T(8,128)S(1)}, f32[512,64]{0,1:T(8,128)}, u32[]{:S(2)}) copy-start(f32[512,64]{0,1:T(8,128)} %param.5) | copy-start | bytes 393220
